TPU v7x, 32 devices: a whole 2x2x4 slice. The times are simulated.
32 devices in a mesh: grid: 16 (over z, y, core), orb: 2 (over x).
Axes of the slice: x: 2, y: 2, z: 4, core: 2. Of those that a mesh axis runs over, the one named last changes fastest.
Arguments:
- density: float32 [32, 3, 128, 128], P('grid', None, 'orb'), may hold values from -4 to 4
- basis_values: float32 [32, 1280, 768], P(('grid', 'orb')), may hold values from -0.5 to 0.5
- quad_weights: float32 [32, 1280], P(('grid', 'orb')), may hold values from 0.01 to 0.1
- ext_potential: float32 [32, 1280], P(('grid', 'orb')), may hold values from 0 to 4
- batch_blocks: int32 [32, 6], P(('grid', 'orb')), may hold values from 0 to 31, as said below
- domain_blocks: int32 [64, 4], P(('grid', 'orb')), may hold values from 0 to 31, as said below
- coefficients: float32 [64, 4, 128, 128], P(('grid', 'orb')), may hold values from -0.25 to 0.25
Outputs:
- density_out: float32 [32, 3, 128, 128], P('grid', None, 'orb')
- coefficients_out: float32 [64, 4, 128, 128], P(('grid', 'orb'))
Inputs may be any that keep to these rules, and one draw needn't show every extreme that they name: `batch_blocks`: the batches on grid index g (batch numbers g * 32 / 16 onward) list the 6 blocks from (g - 1) * 2 onward, taken modulo 32, each once, in some order. `domain_blocks`: the domains on grid index g list 4 distinct blocks among the 6 blocks from (g - 1) * 2 onward, taken modulo 32, at least one of the first 2 and one of the last 2 of them.
All inputs are finite; a program needn't handle non-finite values.
Results may differ from a plain program's by a relative error of at most 0.0003.
Values sent between devices are 32-bit elements; how exact they have to be, the bound alone decides.
No kernel may reach another device: no remote copies, remote signals or barrier semaphores. Data moves between devices by JAX's collectives and lax.ppermute only.
A program may use at most 64 MiB of HBM per device.

v0:
```python
import functools
import jax
import jax.numpy as jnp
from jax import lax
from jax.experimental import pallas as pl
from jax.experimental.pallas import tpu as pltpu
from jax.sharding import PartitionSpec as P

ITERS = 2
step_scale = 0.5

NB = 128
SB = 2 * NB
TILE = 8
HALF = NB // 2
PACKED = NB + TILE
VMEM_BYTES = 40 * 1024 * 1024
POINT_CHUNK = 256
f32 = jnp.float32
bf16 = jnp.bfloat16

LOW = slice(0, PACKED)
HIGH = slice(PACKED + HALF, 2 * PACKED + HALF)
A_ROWS = 2 * PACKED + HALF
B_ROWS = 2 * NB + HALF
PAIR = PACKED + NB
GIVE_ROWS = PAIR + HALF
FINAL_ROWS = PAIR + NB


def split(value):
    high = value.astype(bf16)
    return high, (value - high.astype(f32)).astype(bf16)


def dot3(left, right, contract=((1,), (0,))):
    def one(a, b):
        return lax.dot_general(a, b, (contract, ((), ())), preferred_element_type=f32)

    return one(left[0], right[0]) + (one(left[0], right[1]) + one(left[1], right[0]))


def both(pair, *index):
    return pair[0][index], pair[1][index]


def row_col():
    rows = lax.broadcasted_iota(jnp.int32, (NB, NB), 0)
    return rows, lax.broadcasted_iota(jnp.int32, (NB, NB), 1)


def aligned(value, unit):
    return pl.multiple_of(value * unit, unit)


def core_of():
    return lax.rem(lax.axis_index("grid"), 2)


def relative(block, total_blocks):
    anchor = (lax.axis_index("grid") - 1) * 2
    return lax.rem(block - anchor + total_blocks, total_blocks)


def whole_call(kernel, outs, scratch, name, smem=(), count=0, flops=0, moved=0):
    specs = [
        pl.BlockSpec(memory_space=pltpu.SMEM if i in smem else pltpu.VMEM) for i in range(count)
    ]
    return pl.pallas_call(
        kernel,
        out_shape=[jax.ShapeDtypeStruct(shape, kind) for shape, kind in outs],
        in_specs=specs,
        out_specs=[pl.BlockSpec(memory_space=pltpu.VMEM) for _ in outs],
        scratch_shapes=scratch,
        compiler_params=pltpu.CompilerParams(vmem_limit_bytes=VMEM_BYTES),
        cost_estimate=pl.CostEstimate(flops=flops, bytes_accessed=moved, transcendentals=0),
        name=name,
    )


def sort_kernel(total_blocks, blocks, basis, th, tl, nh, nl):
    for j in range(6):
        at = aligned(relative(blocks[0, j], total_blocks), NB)
        column = basis[:, j * NB : (j + 1) * NB]
        nh[:, pl.ds(at, NB)], nl[:, pl.ds(at, NB)] = split(column)
        th[pl.ds(at, NB), :], tl[pl.ds(at, NB), :] = split(column.T)


def pack_pair(pair_ref, at):
    rows, cols = row_col()
    first = pair_ref[at, :NB, :NB]
    last = pair_ref[at, NB:, NB:]
    merged = jnp.where(rows <= cols, first, last)
    diagonal = jnp.sum(jnp.where(rows == cols, last, 0.0), axis=0, keepdims=True)
    return merged, jnp.broadcast_to(diagonal, (TILE, NB)), pair_ref[at, :NB, NB:]


def store_packed(pair_ref, cross_ref, out_a, out_b, give, keep):
    core = core_of()
    for at, a_at, b_at in ((core, 0, 0), (core + 1, PACKED + HALF, NB + HALF)):
        merged, diagonal, off = pack_pair(pair_ref, at)
        out_a[a_at : a_at + NB, :] = merged
        out_a[a_at + NB : a_at + PACKED, :] = diagonal
        out_b[b_at : b_at + NB, :] = off
    out_a[PACKED : PACKED + HALF, :] = cross_ref[core, :HALF, :]
    out_b[NB : NB + HALF, :] = cross_ref[core, HALF:, :]
    merged, diagonal, off = pack_pair(pair_ref, 2 - 2 * core)
    give[:NB, :] = merged
    give[NB:PACKED, :] = diagonal
    give[PACKED:PAIR, :] = off
    give[PAIR:, :] = cross_ref[1 - core, pl.ds(aligned(1 - core, HALF), HALF), :]
    keep[...] = cross_ref[1 - core, pl.ds(aligned(core, HALF), HALF), :]


def store_final(pair_ref, cross_ref, near, keep, give, edge):
    core = core_of()
    places = ((1, near), (2 - 2 * core, give), (2 * core, edge))
    for at, target in places:
        merged, diagonal, off = pack_pair(pair_ref, at)
        target[:NB, :] = merged
        target[NB:PACKED, :] = diagonal
        target[PACKED:PAIR, :] = off
    give[PAIR:, :] = cross_ref[1 - core]
    keep[...] = cross_ref[1 - core]
    edge[PAIR:, :] = cross_ref[core]


def load_packed(side_a, side_b, mid, other):
    core = core_of()
    pairs = [
        (core, side_a[:NB, :], side_a[NB : NB + 1, :], side_b[:NB, :]),
        (
            core + 1,
            side_a[PACKED + HALF : PACKED + HALF + NB, :],
            side_a[PACKED + HALF + NB : PACKED + HALF + NB + 1, :],
            side_b[NB + HALF :, :],
        ),
        (2 - 2 * core, other[:NB, :], other[NB : NB + 1, :], other[PACKED:PAIR, :]),
    ]
    return core, pairs


def load_cross(cross_ref, core, side_a, side_b, mid, other):
    cross_ref[core, :HALF, :] = side_a[PACKED : PACKED + HALF, :]
    cross_ref[core, HALF:, :] = side_b[NB : NB + HALF, :]
    cross_ref[1 - core, pl.ds(aligned(core, HALF), HALF), :] = mid[...]
    cross_ref[1 - core, pl.ds(aligned(1 - core, HALF), HALF), :] = other[PAIR:, :]


def unpack_pair(merged, diagonal):
    rows, cols = row_col()
    turned = merged.T
    first = jnp.where(rows <= cols, merged, turned)
    last = jnp.where(rows > cols, merged, jnp.where(rows < cols, turned, diagonal))
    return first, last


def fock_body(weights, external, basis_t, basis_n, pairs_ref, terms, scaled, pair_ref, cross_ref):
    points = weights.shape[1]
    pairs = [split(pairs_ref[j]) for j in range(3)]
    terms = [(row, col, split(value)) for row, col, value in terms]
    for start in range(0, points, POINT_CHUNK):
        cols = slice(start, start + POINT_CHUNK)

        def value_of(low, count):
            piece = both(basis_t, slice(low * NB, (low + count) * NB), cols)
            return piece, piece[0].astype(f32) + piece[1].astype(f32)

        rho = jnp.zeros((1, POINT_CHUNK), f32)
        for j in range(3):
            piece, value = value_of(2 * j, 2)
            rho = rho + jnp.sum(dot3(pairs[j], piece) * value, axis=0, keepdims=True)
        for row, col, matrix in terms:
            piece, _ = value_of(col, 1)
            _, value = value_of(row, 1)
            rho = rho + jnp.sum(dot3(matrix, piece) * value, axis=0, keepdims=True)
        potential = external[:, cols] - jnp.exp(jnp.log(rho * rho + 1.0) * (1.0 / 6.0))
        scale = weights[:, cols] * potential
        for j in range(3):
            _, value = value_of(2 * j, 2)
            high, low = split(value * scale)
            scaled[0][2 * j * NB : 2 * (j + 1) * NB, cols] = high
            scaled[1][2 * j * NB : 2 * (j + 1) * NB, cols] = low
    for j in range(3):
        first = 2 * j * NB - (NB if j else 0)
        left = both(scaled, slice(first, 2 * (j + 1) * NB), slice(None))
        block = dot3(left, both(basis_n, slice(None), slice(2 * j * NB, 2 * (j + 1) * NB)))
        if j:
            cross_ref[j - 1] = block[:NB, :NB]
            pair_ref[j] = block[NB:, :]
        else:
            pair_ref[j] = block


def fock_first(
    weights, external, th, tl, nh, nl, own, edge, other,
    out_a, out_b, give, keep, dens, sh, sl, pair_ref, cross_ref,
):
    core = core_of()
    for i in range(2):
        for j in range(2):
            index = 3 * i + j - i + 1
            rows, cols = slice(i * NB, (i + 1) * NB), slice(j * NB, (j + 1) * NB)
            dens[1, rows, cols] = own[index]
            dens[2 * core, rows, cols] = edge[index - 1 + core]
            dens[2 - 2 * core, rows, cols] = other[index]
    low = jnp.where(core == 0, edge[4], other[5])
    high = jnp.where(core == 0, other[0], edge[0])
    terms = [(1, 2, low), (2, 1, own[0]), (3, 4, own[5]), (4, 3, high)]
    fock_body(
        weights, external, (th, tl), (nh, nl), dens, terms, (sh, sl), pair_ref, cross_ref
    )
    store_packed(pair_ref, cross_ref, out_a, out_b, give, keep)


def fock_later(
    weights, external, th, tl, nh, nl, side_a, side_b, mid, other,
    out_a, out_b, give, keep, dens, sh, sl, pair_ref, cross_ref,
):
    rows, cols = row_col()
    core, pairs = load_packed(side_a, side_b, mid, other)
    for at, merged, diagonal, off in pairs:
        twice = merged * 2.0
        dens[at, :NB, :NB] = jnp.where(rows < cols, twice, jnp.where(rows == cols, merged, 0.0))
        dens[at, NB:, NB:] = jnp.where(rows > cols, twice, jnp.where(rows == cols, diagonal, 0.0))
        dens[at, :NB, NB:] = off * 2.0
        dens[at, NB:, :NB] = jnp.zeros((NB, NB), f32)
    load_cross(cross_ref, core, side_a, side_b, mid, other)
    terms = [(1, 2, cross_ref[0] * 2.0), (3, 4, cross_ref[1] * 2.0)]
    fock_body(
        weights, external, (th, tl), (nh, nl), dens, terms, (sh, sl), pair_ref, cross_ref
    )
    store_packed(pair_ref, cross_ref, out_a, out_b, give, keep)


def domain_body(
    total_blocks, lists, coef, side_a, side_b, mid, other,
    fh, fl, gradient, moved, pair_ref, cross_ref,
):
    core, pairs = load_packed(side_a, side_b, mid, other)
    load_cross(cross_ref, core, side_a, side_b, mid, other)
    for at, merged, diagonal, off in pairs:
        first, last = unpack_pair(merged, diagonal)
        pair_ref[at, :NB, :NB] = first
        pair_ref[at, :NB, NB:] = off
        pair_ref[at, NB:, :NB] = off.T
        pair_ref[at, NB:, NB:] = last
    zero = jnp.zeros((NB, NB), f32)
    between = [(cross_ref[j], cross_ref[j].T) for j in range(2)]
    for j in range(3):
        top = NB if j else 0
        slab = [pair_ref[j]]
        if j:
            slab = [jnp.concatenate([between[j - 1][0], zero], axis=1)] + slab
        if j < 2:
            slab = slab + [jnp.concatenate([zero, between[j][1]], axis=1)]
        slab = jnp.concatenate(slab, axis=0)
        start = 2 * j * NB - top
        stop = start + slab.shape[0]
        product = dot3(split(slab), split(coef[2 * j * NB : 2 * (j + 1) * NB, :]))
        if j == 0:
            gradient[start:stop, :] = product
        else:
            seen = (2 * j + 1) * NB
            gradient[start:seen, :] += product[: seen - start]
            gradient[seen:stop, :] = product[seen - start :]
    domains = len(lists)
    mixed = []
    for d in range(domains):
        cols = slice(d * NB, (d + 1) * NB)
        mixed.append(dot3(split(coef[:, cols]), split(gradient[:, cols]), ((0,), (0,))))
    for d in range(0, domains, 2):
        cols = slice(d * NB, (d + 2) * NB)
        square = jnp.concatenate(
            [
                jnp.concatenate([mixed[d], zero], axis=1),
                jnp.concatenate([zero, mixed[d + 1]], axis=1),
            ],
            axis=0,
        )
        moved[:, cols] = dot3(split(coef[:, cols]), split(square))


def new_rows(total_blocks, lists, coef, gradient, moved):
    for d, (blocks, row) in enumerate(lists):
        cols = slice(d * NB, (d + 1) * NB)
        for i in range(4):
            at = aligned(relative(blocks[row, i], total_blocks), NB)
            rows = pl.ds(at, NB)
            value = coef[rows, cols] - step_scale * (gradient[rows, cols] - moved[rows, cols])
            yield d, i, rows, cols, value


def density_body(coef, pair_ref, cross_ref):
    pieces = split(coef[...])
    contract = ((1,), (1,))
    for j in range(3):
        piece = both(pieces, slice(2 * j * NB, 2 * (j + 1) * NB))
        pair_ref[j] = dot3(piece, piece, contract)
    for j in range(2):
        first = both(pieces, slice((2 * j + 1) * NB, (2 * j + 2) * NB))
        last = both(pieces, slice((2 * j + 2) * NB, (2 * j + 3) * NB))
        cross_ref[j] = dot3(first, last, contract)


def domain_first(
    total_blocks, own_lists, other_lists, own, partner, side_a, side_b, mid, other,
    coef_out, out_a, out_b, give, keep, coef, gradient, moved, pair_ref, cross_ref,
):
    lists = [(own_lists, 0), (own_lists, 1), (other_lists, 0), (other_lists, 1)]
    coef[...] = jnp.zeros_like(coef)
    for d, (blocks, row) in enumerate(lists):
        source = own if d < 2 else partner
        for i in range(4):
            at = aligned(relative(blocks[row, i], total_blocks), NB)
            coef[pl.ds(at, NB), d * NB : (d + 1) * NB] = source[row, i]
    domain_body(
        total_blocks, lists, coef, side_a, side_b, mid, other,
        None, None, gradient, moved, pair_ref, cross_ref,
    )
    coef_out[...] = jnp.zeros_like(coef_out)
    for _, _, rows, cols, value in new_rows(total_blocks, lists, coef, gradient, moved):
        coef_out[rows, cols] = value
    density_body(coef_out, pair_ref, cross_ref)
    store_packed(pair_ref, cross_ref, out_a, out_b, give, keep)


def domain_last(
    total_blocks, own_lists, other_lists, coef, side_a, side_b, mid, other,
    result, near, keep, give, edge, fresh, gradient, moved, pair_ref, cross_ref,
):
    lists = [(own_lists, 0), (own_lists, 1), (other_lists, 0), (other_lists, 1)]
    domain_body(
        total_blocks, lists, coef, side_a, side_b, mid, other,
        None, None, gradient, moved, pair_ref, cross_ref,
    )
    fresh[...] = jnp.zeros_like(fresh)
    for d, i, rows, cols, value in new_rows(total_blocks, lists, coef, gradient, moved):
        fresh[rows, cols] = value
        if d < 2:
            result[d, i] = value
    density_body(fresh, pair_ref, cross_ref)
    store_final(pair_ref, cross_ref, near, keep, give, edge)


def owner_kernel(near, keep, edge, from_core, from_edge, out, full):
    core = core_of()
    total = near[...] + from_core[:PAIR, :] + from_edge[:PAIR, :]
    first, last = unpack_pair(total[:NB], total[NB : NB + 1])
    off = total[PACKED:PAIR]
    mid = keep[...] + from_core[PAIR:, :]
    side = edge[PAIR:, :] + from_edge[PAIR:, :]
    below = jnp.where(core == 0, side, mid)
    above = jnp.where(core == 0, mid, side)
    full[0, 0] = below.T
    full[0, 1] = first
    full[0, 2] = off
    full[1, 0] = off.T
    full[1, 1] = last
    full[1, 2] = above
    start = aligned(lax.axis_index("orb"), HALF)
    for i in range(2):
        for s in range(3):
            out[i, s] = full[i, s, pl.ds(start, HALF), :]


def to_core(value):
    count = lax.axis_size("grid")
    return lax.ppermute(value, "grid", [(i, i ^ 1) for i in range(count)])


def to_edge(value):
    count = lax.axis_size("grid")
    route = [(i, (i + 1) % count if i % 2 else (i - 1) % count) for i in range(count)]
    return lax.ppermute(value, "grid", route)


def to_orb(value):
    return lax.ppermute(value, "orb", [(0, 1), (1, 0)])


def add_near(core, side_a, side_b, keep, arrived):
    packed, off = arrived[:PACKED], arrived[PACKED:PAIR]

    def placed(piece, gap):
        zero = jnp.zeros_like(piece)
        parts = [
            jnp.where(core == 1, piece, zero),
            jnp.zeros((gap, NB), f32),
            jnp.where(core == 0, piece, zero),
        ]
        return jnp.concatenate(parts, axis=0)

    return side_a + placed(packed, HALF), side_b + placed(off, HALF), keep + arrived[PAIR:]


def near_part(core, side_a, side_b, mid):
    packed = lax.dynamic_slice_in_dim(side_a, (1 - core) * (PACKED + HALF), PACKED, 0)
    off = lax.dynamic_slice_in_dim(side_b, (1 - core) * (NB + HALF), NB, 0)
    return jnp.concatenate([packed, off, mid], axis=0)


def total_over_all(core, side_a, side_b, give, keep):
    side_a, side_b, keep = add_near(core, side_a, side_b, keep, to_core(give))
    first_a = to_orb(side_a)
    first_b = to_edge(side_b)
    side_a = side_a + first_a
    side_b = side_b + first_b
    last_a = to_edge(side_a)
    last_b = to_orb(jnp.concatenate([side_b, keep], axis=0))
    side_a = side_a + last_a
    side_b = side_b + last_b[:B_ROWS]
    keep = keep + last_b[B_ROWS:]
    return side_a, side_b, keep, to_core(near_part(core, side_a, side_b, keep))


def total_over_grid(core, side_a, side_b, give, keep):
    side_a, side_b, keep = add_near(core, side_a, side_b, keep, to_core(give))
    arrived = to_edge(jnp.concatenate([side_a, side_b], axis=0))
    side_a = side_a + arrived[:A_ROWS]
    side_b = side_b + arrived[A_ROWS:]
    return side_a, side_b, keep, to_core(near_part(core, side_a, side_b, keep))


def shards(
    density, basis_values, quad_weights, ext_potential, batch_blocks, domain_blocks, coefficients
):
    total_blocks = density.shape[0] * lax.axis_size("grid")
    points = basis_values.shape[1]
    core = lax.rem(lax.axis_index("grid"), 2)
    window = 6 * NB
    half_shape, full_shape = (points, window), (window, points)
    packed_outs = [((A_ROWS, NB), f32), ((B_ROWS, NB), f32), ((GIVE_ROWS, NB), f32), ((HALF, NB), f32)]
    band_scratch = [pltpu.VMEM((3, SB, SB), f32), pltpu.VMEM((2, NB, NB), f32)]

    basis = whole_call(
        functools.partial(sort_kernel, total_blocks),
        [(full_shape, bf16)] * 2 + [(half_shape, bf16)] * 2,
        [],
        "sort_basis",
        smem=(0,),
        count=2,
        moved=12 * points * window,
    )(batch_blocks, basis_values[0])

    partner = to_orb(density)
    first_half = lax.axis_index("orb") == 0
    own = jnp.concatenate(
        [jnp.where(first_half, density, partner), jnp.where(first_half, partner, density)], axis=2
    ).reshape(6, NB, NB)
    from_edge = to_edge(lax.dynamic_slice_in_dim(own, core, 5, 0))
    from_core = to_core(own)
    coefficients_ready, own = lax.optimization_barrier((coefficients, own))
    other_coefficients = to_orb(coefficients_ready)
    other_lists = to_orb(domain_blocks)

    fock_scratch = [
        pltpu.VMEM((3, SB, SB), f32),
        pltpu.VMEM(full_shape, bf16),
        pltpu.VMEM(full_shape, bf16),
    ] + band_scratch
    domain_scratch = [pltpu.VMEM((window, 4 * NB), f32)] * 2 + band_scratch
    fock_cost = 2 * 3 * 8 * points * SB * SB

    coef = None
    packed = None
    for iteration in range(ITERS):
        if iteration == 0:
            kernel, operands = fock_first, (own, from_edge, from_core)
        else:
            kernel, operands = fock_later, packed
        made = whole_call(
            kernel, packed_outs, fock_scratch, "fock", count=6 + len(operands), flops=fock_cost
        )(quad_weights, ext_potential, *basis, *operands)
        packed = total_over_all(core, *made)
        if iteration < ITERS - 1:
            if iteration == 0:
                outs = [((window, 4 * NB), f32)] + packed_outs
                coef, *made = whole_call(
                    functools.partial(domain_first, total_blocks),
                    outs,
                    [pltpu.VMEM((window, 4 * NB), f32)] + domain_scratch,
                    "domains",
                    smem=(0, 1),
                    count=8,
                    flops=fock_cost // 2,
                )(domain_blocks, other_lists, coefficients, other_coefficients, *packed)
            packed = total_over_grid(core, *made)
        else:
            outs = [(coefficients.shape, f32), ((PAIR, NB), f32), ((NB, NB), f32)] + [
                ((FINAL_ROWS, NB), f32)
            ] * 2
            result, near, keep, give, edge = whole_call(
                functools.partial(domain_last, total_blocks),
                outs,
                [pltpu.VMEM((window, 4 * NB), f32)] + domain_scratch,
                "domains_last",
                smem=(0, 1),
                count=7,
                flops=fock_cost // 2,
            )(domain_blocks, other_lists, coef, *packed)
            arrived_edge = to_edge(edge)
            arrived_core = to_core(give)
            (rows,) = whole_call(
                owner_kernel,
                [(density.shape, f32)],
                [pltpu.VMEM((2, 3, NB, NB), f32)],
                "owner_rows",
                count=5,
            )(near, keep, edge, arrived_core, arrived_edge)
    return (rows, result)


def solution(mesh):
    in_specs = (
        P("grid", None, "orb", None),
        P(("grid", "orb"), None, None),
        P(("grid", "orb"), None),
        P(("grid", "orb"), None),
        P(("grid", "orb"), None),
        P(("grid", "orb"), None),
        P(("grid", "orb"), None, None, None),
    )
    out_specs = (P("grid", None, "orb", None), P(("grid", "orb"), None, None, None))
    return jax.shard_map(shards, mesh=mesh, in_specs=in_specs, out_specs=out_specs, check_vma=False)
```

profile of v0, /device:TPU:0, one launch (start us, length us, event | category | flops | bytes accessed | tf_op | source)
XLA Modules:
  0.0 112.4 jit_solution(8556533048766455091)
XLA Ops:
  0.6 3.0 %collective-permute-start.1 = (f32[2,3,64,128]{3,2,1,0:T(8,128)}, f32[2,3,64,128]{3,2,1,0:T(8,128)S(1)}, u32[]{:S(2)}, u32[]{:S(2)}) collective-permute-start(f32[2,3,64,128]{3,2,1,0:T(8,128)} %param.7), channel_id=1, source_target_pairs={{0,1},{1,0},{2,3},{3,2},{4,5},{5,4},{6,7},{7,6},{8,9},{9,8},{10,11... | collective-permute-start | bytes 589832 | tf_op jit(solution)/shard_map/ppermute | solution.py:379
  3.6 5.1 %collective-permute-done.1 = f32[2,3,64,128]{3,2,1,0:T(8,128)S(1)} collective-permute-done((f32[2,3,64,128]{3,2,1,0:T(8,128)}, f32[2,3,64,128]{3,2,1,0:T(8,128)S(1)}, u32[]{:S(2)}, u32[]{:S(2)}) %collective-permute-start.1) | collective-permute-done | bytes 196640 | tf_op jit(solution)/shard_map/ppermute | solution.py:379
  8.8 1.0 broadcast_select_fusion.1
  9.8 0.1 collective-permute-start.4
  9.9 5.0 %collective-permute-start.3 = (f32[5,128,128]{2,1,0:T(8,128)S(1)}, f32[5,128,128]{2,1,0:T(8,128)S(1)}, u32[]{:S(2)}, u32[]{:S(2)}) collective-permute-start(f32[5,128,128]{2,1,0:T(8,128)S(1)} %constant_dynamic-slice_fusion.6), channel_id=1, source_target_pairs={{0,30},{2,4},{4,2},{6,8},{8,6},{10,12},{12,10},{14,16},{16,14},{18... | collective-permute-start | bytes 983048 | tf_op jit(solution)/shard_map/ppermute | solution.py:375
  14.8 2.1 %copy-done = f32[1,1280,768]{2,1,0:T(8,128)S(1)} copy-done((f32[1,1280,768]{2,1,0:T(8,128)S(1)}, f32[1,1280,768]{2,1,0:T(8,128)}, u32[]{:S(2)}) %copy-start) | copy-done | bytes 3932184
  17.0 1.7 %sort_basis.1 = (bf16[768,1280]{1,0:T(8,128)(2,1)S(1)}, bf16[768,1280]{1,0:T(8,128)(2,1)S(1)}, bf16[1280,768]{1,0:T(8,128)(2,1)S(1)}, bf16[1280,768]{1,0:T(8,128)(2,1)S(1)}) custom-call(s32[1,6]{1,0:T(1,128)S(1)} %copy-done.1, f32[1280,768]{1,0:T(8,128)S(1)} %bitcast.2), custom_call_target="tpu_custom_call" | custom-call | bytes 11796480 | tf_op jit(solution)/shard_map/sort_basis/pallas_call | solution.py:436
  18.7 1.0 collective-permute-done.3.edge
  19.7 5.4 %fock.2 = (f32[336,128]{1,0:T(8,128)S(1)}, f32[320,128]{1,0:T(8,128)S(1)}, f32[328,128]{1,0:T(8,128)S(1)}, f32[64,128]{1,0:T(8,128)S(1)}) custom-call(f32[1,1280]{1,0:T(1,128)S(1)} %copy-done.9, f32[1,1280]{1,0:T(1,128)S(1)} %copy-done.10, bf16[768,1280]{1,0:T(8,128)(2,1)S(1)} %get-tuple-element.27.th, bf16[768,1280]{1,0:T(8,128)(2,1)S(1)} %get-tuple-element.28.tl, ...), custom_call_target="tpu_custom_call" | custom-call | flops 4026531840 | tf_op jit(solution)/shard_map/fock/pallas_call | solution.py:472
  25.1 0.8 collective-permute-start.5
  26.0 1.0 collective-permute-done.5
  27.1 4.5 %collective-permute-start.8 = (f32[320,128]{1,0:T(8,128)S(1)}, f32[320,128]{1,0:T(8,128)S(1)}, u32[]{:S(2)}, u32[]{:S(2)}) collective-permute-start(f32[320,128]{1,0:T(8,128)S(1)} %fusion.7), channel_id=1, source_target_pairs={{0,30},{2,4},{4,2},{6,8},{8,6},{10,12},{12,10},{14,16},{16,14},{18... | collective-permute-start | bytes 491528 | tf_op jit(solution)/shard_map/ppermute | solution.py:375
  31.6 1.6 %collective-permute-start.6 = (f32[336,128]{1,0:T(8,128)S(1)}, f32[336,128]{1,0:T(8,128)S(1)}, u32[]{:S(2)}, u32[]{:S(2)}) collective-permute-start(f32[336,128]{1,0:T(8,128)S(1)} %fusion.1), channel_id=1, source_target_pairs={{0,1},{1,0},{2,3},{3,2},{4,5},{5,4},{6,7},{7,6},{8,9},{9,8},{10,11... | collective-permute-start | bytes 516104 | tf_op jit(solution)/shard_map/ppermute | solution.py:379
  33.2 1.4 %collective-permute-done.8 = f32[320,128]{1,0:T(8,128)S(1)} collective-permute-done((f32[320,128]{1,0:T(8,128)S(1)}, f32[320,128]{1,0:T(8,128)S(1)}, u32[]{:S(2)}, u32[]{:S(2)}) %collective-permute-start.8) | collective-permute-done | bytes 163872 | tf_op jit(solution)/shard_map/ppermute | solution.py:375
  34.6 2.5 %collective-permute-done.6 = f32[336,128]{1,0:T(8,128)S(1)} collective-permute-done((f32[336,128]{1,0:T(8,128)S(1)}, f32[336,128]{1,0:T(8,128)S(1)}, u32[]{:S(2)}, u32[]{:S(2)}) %collective-permute-start.6) | collective-permute-done | bytes 172064 | tf_op jit(solution)/shard_map/ppermute | solution.py:379
  37.1 2.0 %collective-permute-start.7 = (f32[336,128]{1,0:T(8,128)S(1)}, f32[336,128]{1,0:T(8,128)}, u32[]{:S(2)}, u32[]{:S(2)}) collective-permute-start(f32[336,128]{1,0:T(8,128)S(1)} %add.78), channel_id=1, source_target_pairs={{0,30},{2,4},{4,2},{6,8},{8,6},{10,12},{12,10},{14,16},{16,14},{18... | collective-permute-start | bytes 516104 | tf_op jit(solution)/shard_map/ppermute | solution.py:375
  39.1 1.6 %collective-permute-start.9 = (f32[384,128]{1,0:T(8,128)S(1)}, f32[384,128]{1,0:T(8,128)S(1)}, u32[]{:S(2)}, u32[]{:S(2)}) collective-permute-start(f32[384,128]{1,0:T(8,128)S(1)} %pad_maximum_fusion.8), channel_id=1, source_target_pairs={{0,1},{1,0},{2,3},{3,2},{4,5},{5,4},{6,7},{7,6},{8,9},{9,8},{10,11... | collective-permute-start | bytes 589832 | tf_op jit(solution)/shard_map/ppermute | solution.py:379
  40.7 0.5 collective-permute-start.2
  41.2 3.6 %collective-permute-done.7 = f32[336,128]{1,0:T(8,128)} collective-permute-done((f32[336,128]{1,0:T(8,128)S(1)}, f32[336,128]{1,0:T(8,128)}, u32[]{:S(2)}, u32[]{:S(2)}) %collective-permute-start.7) | collective-permute-done | bytes 172064 | tf_op jit(solution)/shard_map/ppermute | solution.py:375
  44.8 0.9 add.79.side_a
  45.8 1.3 %collective-permute-done.9 = f32[384,128]{1,0:T(8,128)S(1)} collective-permute-done((f32[384,128]{1,0:T(8,128)S(1)}, f32[384,128]{1,0:T(8,128)S(1)}, u32[]{:S(2)}, u32[]{:S(2)}) %collective-permute-start.9) | collective-permute-done | bytes 196640 | tf_op jit(solution)/shard_map/ppermute | solution.py:379
  47.2 1.6 %collective-permute-start = (s32[2,4]{1,0:T(2,128)S(1)}, s32[2,4]{1,0:T(2,128)S(1)}, u32[]{:S(2)}, u32[]{:S(2)}) collective-permute-start(s32[2,4]{1,0:T(2,128)S(1)} %copy-done.11), channel_id=1, source_target_pairs={{0,1},{1,0},{2,3},{3,2},{4,5},{5,4},{6,7},{7,6},{8,9},{9,8},{10,11... | collective-permute-start | bytes 104 | tf_op jit(solution)/shard_map/ppermute | solution.py:379
  48.8 5.9 %collective-permute-done.other_lists = s32[2,4]{1,0:T(2,128)S(1)} collective-permute-done((s32[2,4]{1,0:T(2,128)S(1)}, s32[2,4]{1,0:T(2,128)S(1)}, u32[]{:S(2)}, u32[]{:S(2)}) %collective-permute-start) | collective-permute-done | bytes 64 | tf_op jit(solution)/shard_map/ppermute | solution.py:379
  54.7 5.3 %domains.1 = (f32[768,512]{1,0:T(8,128)S(1)}, f32[336,128]{1,0:T(8,128)S(1)}, f32[320,128]{1,0:T(8,128)S(1)}, f32[328,128]{1,0:T(8,128)S(1)}, f32[64,128]{1,0:T(8,128)S(1)}) custom-call(s32[2,4]{1,0:T(2,128)S(1)} %copy-done.11, s32[2,4]{1,0:T(2,128)S(1)} %collective-permute-done.other_lists, f32[2,4,128,128]{3,2,1,0:T(8,128)S(1)} %copy-done.8, ...), custom_call_target="tpu_custom_call" | custom-call | flops 2013265920 | tf_op jit(solution)/shard_map/domains/pallas_call | solution.py:479
  60.1 0.1 collective-permute-start.11
  60.2 1.4 %collective-permute-done.11 = f32[328,128]{1,0:T(8,128)S(1)} collective-permute-done((f32[328,128]{1,0:T(8,128)S(1)}, f32[328,128]{1,0:T(8,128)S(1)}, u32[]{:S(2)}, u32[]{:S(2)}) %collective-permute-start.11) | collective-permute-done | bytes 167968 | tf_op jit(solution)/shard_map/ppermute | solution.py:369
  61.7 3.7 %collective-permute-start.12 = (f32[656,128]{1,0:T(8,128)S(1)}, f32[656,128]{1,0:T(8,128)S(1)}, u32[]{:S(2)}, u32[]{:S(2)}) collective-permute-start(f32[656,128]{1,0:T(8,128)S(1)} %pad_maximum_fusion.1), channel_id=1, source_target_pairs={{0,30},{2,4},{4,2},{6,8},{8,6},{10,12},{12,10},{14,16},{16,14},{18... | collective-permute-start | bytes 1007624 | tf_op jit(solution)/shard_map/ppermute | solution.py:375
  65.4 5.8 %collective-permute-done.12 = f32[656,128]{1,0:T(8,128)S(1)} collective-permute-done((f32[656,128]{1,0:T(8,128)S(1)}, f32[656,128]{1,0:T(8,128)S(1)}, u32[]{:S(2)}, u32[]{:S(2)}) %collective-permute-start.12) | collective-permute-done | bytes 335904 | tf_op jit(solution)/shard_map/ppermute | solution.py:375
  71.3 1.0 collective-permute-start.13
  72.3 1.0 collective-permute-done.13.other
  73.3 5.1 %fock.3 = (f32[336,128]{1,0:T(8,128)S(1)}, f32[320,128]{1,0:T(8,128)S(1)}, f32[328,128]{1,0:T(8,128)S(1)}, f32[64,128]{1,0:T(8,128)S(1)}) custom-call(f32[1,1280]{1,0:T(1,128)S(1)} %copy-done.9, f32[1,1280]{1,0:T(1,128)S(1)} %copy-done.10, bf16[768,1280]{1,0:T(8,128)(2,1)S(1)} %get-tuple-element.27.th, bf16[768,1280]{1,0:T(8,128)(2,1)S(1)} %copy-done.3, ...), custom_call_target="tpu_custom_call" | custom-call | flops 4026531840 | tf_op jit(solution)/shard_map/fock/pallas_call | solution.py:472
  78.4 0.5 collective-permute-start.14
  78.9 1.0 collective-permute-done.14
  80.0 3.7 %collective-permute-start.17 = (f32[320,128]{1,0:T(8,128)S(1)}, f32[320,128]{1,0:T(8,128)S(1)}, u32[]{:S(2)}, u32[]{:S(2)}) collective-permute-start(f32[320,128]{1,0:T(8,128)S(1)} %fusion.11), channel_id=1, source_target_pairs={{0,30},{2,4},{4,2},{6,8},{8,6},{10,12},{12,10},{14,16},{16,14},{18... | collective-permute-start | bytes 491528 | tf_op jit(solution)/shard_map/ppermute | solution.py:375
  83.7 1.6 %collective-permute-start.15 = (f32[336,128]{1,0:T(8,128)S(1)}, f32[336,128]{1,0:T(8,128)S(1)}, u32[]{:S(2)}, u32[]{:S(2)}) collective-permute-start(f32[336,128]{1,0:T(8,128)S(1)} %fusion.5), channel_id=1, source_target_pairs={{0,1},{1,0},{2,3},{3,2},{4,5},{5,4},{6,7},{7,6},{8,9},{9,8},{10,11... | collective-permute-start | bytes 516104 | tf_op jit(solution)/shard_map/ppermute | solution.py:379
  85.2 2.2 %collective-permute-done.17 = f32[320,128]{1,0:T(8,128)S(1)} collective-permute-done((f32[320,128]{1,0:T(8,128)S(1)}, f32[320,128]{1,0:T(8,128)S(1)}, u32[]{:S(2)}, u32[]{:S(2)}) %collective-permute-start.17) | collective-permute-done | bytes 163872 | tf_op jit(solution)/shard_map/ppermute | solution.py:375
  87.5 1.7 %collective-permute-done.15 = f32[336,128]{1,0:T(8,128)S(1)} collective-permute-done((f32[336,128]{1,0:T(8,128)S(1)}, f32[336,128]{1,0:T(8,128)S(1)}, u32[]{:S(2)}, u32[]{:S(2)}) %collective-permute-start.15) | collective-permute-done | bytes 172064 | tf_op jit(solution)/shard_map/ppermute | solution.py:379
  89.2 2.0 %collective-permute-start.16 = (f32[336,128]{1,0:T(8,128)S(1)}, f32[336,128]{1,0:T(8,128)S(1)}, u32[]{:S(2)}, u32[]{:S(2)}) collective-permute-start(f32[336,128]{1,0:T(8,128)S(1)} %add.93), channel_id=1, source_target_pairs={{0,30},{2,4},{4,2},{6,8},{8,6},{10,12},{12,10},{14,16},{16,14},{18... | collective-permute-start | bytes 516104 | tf_op jit(solution)/shard_map/ppermute | solution.py:375
  91.2 1.6 %collective-permute-start.18 = (f32[384,128]{1,0:T(8,128)S(1)}, f32[384,128]{1,0:T(8,128)S(1)}, u32[]{:S(2)}, u32[]{:S(2)}) collective-permute-start(f32[384,128]{1,0:T(8,128)S(1)} %pad_maximum_fusion.9), channel_id=1, source_target_pairs={{0,1},{1,0},{2,3},{3,2},{4,5},{5,4},{6,7},{7,6},{8,9},{9,8},{10,11... | collective-permute-start | bytes 589832 | tf_op jit(solution)/shard_map/ppermute | solution.py:379
  92.8 4.0 %collective-permute-done.16 = f32[336,128]{1,0:T(8,128)S(1)} collective-permute-done((f32[336,128]{1,0:T(8,128)S(1)}, f32[336,128]{1,0:T(8,128)S(1)}, u32[]{:S(2)}, u32[]{:S(2)}) %collective-permute-start.16) | collective-permute-done | bytes 172064 | tf_op jit(solution)/shard_map/ppermute | solution.py:375
  96.8 0.1 collective-permute-done.18
  97.0 0.1 collective-permute-start.19
  97.1 1.4 %collective-permute-done.19.other = f32[328,128]{1,0:T(8,128)S(1)} collective-permute-done((f32[328,128]{1,0:T(8,128)S(1)}, f32[328,128]{1,0:T(8,128)S(1)}, u32[]{:S(2)}, u32[]{:S(2)}) %collective-permute-start.19) | collective-permute-done | bytes 167968 | tf_op jit(solution)/shard_map/ppermute | solution.py:369
  98.5 4.9 %domains_last.1 = (f32[2,4,128,128]{3,2,1,0:T(8,128)}, f32[264,128]{1,0:T(8,128)S(1)}, f32[128,128]{1,0:T(8,128)S(1)}, f32[392,128]{1,0:T(8,128)S(1)}, f32[392,128]{1,0:T(8,128)S(1)}) custom-call(s32[2,4]{1,0:T(2,128)S(1)} %copy-done.11, s32[2,4]{1,0:T(2,128)S(1)} %collective-permute-done.other_lists, f32[768,512]{1,0:T(8,128)S(1)} %get-tuple-element.36.coef, ...), custom_call_target="tpu_custom_call" | custom-call | flops 2013265920 | tf_op jit(solution)/shard_map/domains_last/pallas_call | solution.py:493
  103.5 0.2 collective-permute-start.20
  103.7 2.1 %collective-permute-start.21 = (f32[392,128]{1,0:T(8,128)S(1)}, f32[392,128]{1,0:T(8,128)S(1)}, u32[]{:S(2)}, u32[]{:S(2)}) collective-permute-start(f32[392,128]{1,0:T(8,128)S(1)} %get-tuple-element.47.edge), channel_id=1, source_target_pairs={{0,30},{2,4},{4,2},{6,8},{8,6},{10,12},{12,10},{14,16},{16,14},{18... | collective-permute-start | bytes 602120 | tf_op jit(solution)/shard_map/ppermute | solution.py:375
  105.7 5.8 %collective-permute-done.21.from_edge = f32[392,128]{1,0:T(8,128)S(1)} collective-permute-done((f32[392,128]{1,0:T(8,128)S(1)}, f32[392,128]{1,0:T(8,128)S(1)}, u32[]{:S(2)}, u32[]{:S(2)}) %collective-permute-start.21) | collective-permute-done | bytes 200736 | tf_op jit(solution)/shard_map/ppermute | solution.py:375
  111.5 0.9 owner_rows.1
  (69 shorter events, 0.8 us)
Async XLA Ops:
  0.6 14.2 %copy-start.1 = (s32[1,6]{1,0:T(1,128)S(1)}, s32[1,6]{1,0:T(1,128)}, u32[]{:S(2)}) copy-start(s32[1,6]{1,0:T(1,128)} %blocks.1) | copy-start | bytes 76
  0.6 8.1 %collective-permute-start.1 = (f32[2,3,64,128]{3,2,1,0:T(8,128)}, f32[2,3,64,128]{3,2,1,0:T(8,128)S(1)}, u32[]{:S(2)}, u32[]{:S(2)}) collective-permute-start(f32[2,3,64,128]{3,2,1,0:T(8,128)} %param.7), channel_id=1, source_target_pairs={{0,1},{1,0},{2,3},{3,2},{4,5},{5,4},{6,7},{7,6},{8,9},{9,8},{10,11... | collective-permute-start | bytes 589832 | tf_op jit(solution)/shard_map/ppermute | solution.py:379
  9.8 9.9 %collective-permute-start.4 = (f32[6,128,128]{2,1,0:T(8,128)S(1)}, f32[6,128,128]{2,1,0:T(8,128)S(1)}, u32[]{:S(2)}, u32[]{:S(2)}) collective-permute-start(f32[6,128,128]{2,1,0:T(8,128)S(1)} %bitcast.3), channel_id=1, source_target_pairs={{0,2},{2,0},{4,6},{6,4},{8,10},{10,8},{12,14},{14,12},{16,18},{18,... | collective-permute-start | bytes 1179656 | tf_op jit(solution)/shard_map/ppermute | solution.py:369
  9.9 9.8 %collective-permute-start.3 = (f32[5,128,128]{2,1,0:T(8,128)S(1)}, f32[5,128,128]{2,1,0:T(8,128)S(1)}, u32[]{:S(2)}, u32[]{:S(2)}) collective-permute-start(f32[5,128,128]{2,1,0:T(8,128)S(1)} %constant_dynamic-slice_fusion.6), channel_id=1, source_target_pairs={{0,30},{2,4},{4,2},{6,8},{8,6},{10,12},{12,10},{14,16},{16,14},{18... | collective-permute-start | bytes 983048 | tf_op jit(solution)/shard_map/ppermute | solution.py:375
  14.8 2.1 %copy-start = (f32[1,1280,768]{2,1,0:T(8,128)S(1)}, f32[1,1280,768]{2,1,0:T(8,128)}, u32[]{:S(2)}) copy-start(f32[1,1280,768]{2,1,0:T(8,128)} %param.8) | copy-start | bytes 11796484
  17.0 2.8 %copy-start.9 = (f32[1,1280]{1,0:T(1,128)S(1)}, f32[1,1280]{1,0:T(1,128)}, u32[]{:S(2)}) copy-start(f32[1,1280]{1,0:T(1,128)} %weights.3) | copy-start | bytes 15364
  17.0 2.8 %copy-start.10 = (f32[1,1280]{1,0:T(1,128)S(1)}, f32[1,1280]{1,0:T(1,128)}, u32[]{:S(2)}) copy-start(f32[1,1280]{1,0:T(1,128)} %external.3) | copy-start | bytes 15364
  18.7 6.4 %copy-start.2 = (bf16[768,1280]{1,0:T(8,128)(2,1)}, bf16[768,1280]{1,0:T(8,128)(2,1)S(1)}, u32[]{:S(2)}) copy-start(bf16[768,1280]{1,0:T(8,128)(2,1)S(1)} %get-tuple-element.28.tl) | copy-start | bytes 5898244
  18.7 6.4 %copy-start.4 = (bf16[1280,768]{1,0:T(8,128)(2,1)}, bf16[1280,768]{1,0:T(8,128)(2,1)S(1)}, u32[]{:S(2)}) copy-start(bf16[1280,768]{1,0:T(8,128)(2,1)S(1)} %get-tuple-element.29.nh) | copy-start | bytes 5898244
  18.7 6.4 %copy-start.6 = (bf16[1280,768]{1,0:T(8,128)(2,1)}, bf16[1280,768]{1,0:T(8,128)(2,1)S(1)}, u32[]{:S(2)}) copy-start(bf16[1280,768]{1,0:T(8,128)(2,1)S(1)} %get-tuple-element.30.nl) | copy-start | bytes 5898244
  25.1 15.6 %copy-start.8 = (f32[2,4,128,128]{3,2,1,0:T(8,128)S(1)}, f32[2,4,128,128]{3,2,1,0:T(8,128)}, u32[]{:S(2)}) copy-start(f32[2,4,128,128]{3,2,1,0:T(8,128)} %own.1) | copy-start | bytes 1572868
  25.1 1.9 %collective-permute-start.5 = (f32[328,128]{1,0:T(8,128)S(1)}, f32[328,128]{1,0:T(8,128)S(1)}, u32[]{:S(2)}, u32[]{:S(2)}) collective-permute-start(f32[328,128]{1,0:T(8,128)S(1)} %get-tuple-element.33), channel_id=1, source_target_pairs={{0,2},{2,0},{4,6},{6,4},{8,10},{10,8},{12,14},{14,12},{16,18},{18,... | collective-permute-start | bytes 503816 | tf_op jit(solution)/shard_map/ppermute | solution.py:369
  27.1 20.1 %copy-start.11 = (s32[2,4]{1,0:T(2,128)S(1)}, s32[2,4]{1,0:T(2,128)}, u32[]{:S(2)}) copy-start(s32[2,4]{1,0:T(2,128)} %own_lists.3) | copy-start | bytes 100
  27.1 7.5 %collective-permute-start.8 = (f32[320,128]{1,0:T(8,128)S(1)}, f32[320,128]{1,0:T(8,128)S(1)}, u32[]{:S(2)}, u32[]{:S(2)}) collective-permute-start(f32[320,128]{1,0:T(8,128)S(1)} %fusion.7), channel_id=1, source_target_pairs={{0,30},{2,4},{4,2},{6,8},{8,6},{10,12},{12,10},{14,16},{16,14},{18... | collective-permute-start | bytes 491528 | tf_op jit(solution)/shard_map/ppermute | solution.py:375
  31.6 5.5 %collective-permute-start.6 = (f32[336,128]{1,0:T(8,128)S(1)}, f32[336,128]{1,0:T(8,128)S(1)}, u32[]{:S(2)}, u32[]{:S(2)}) collective-permute-start(f32[336,128]{1,0:T(8,128)S(1)} %fusion.1), channel_id=1, source_target_pairs={{0,1},{1,0},{2,3},{3,2},{4,5},{5,4},{6,7},{7,6},{8,9},{9,8},{10,11... | collective-permute-start | bytes 516104 | tf_op jit(solution)/shard_map/ppermute | solution.py:379
  37.1 7.7 %collective-permute-start.7 = (f32[336,128]{1,0:T(8,128)S(1)}, f32[336,128]{1,0:T(8,128)}, u32[]{:S(2)}, u32[]{:S(2)}) collective-permute-start(f32[336,128]{1,0:T(8,128)S(1)} %add.78), channel_id=1, source_target_pairs={{0,30},{2,4},{4,2},{6,8},{8,6},{10,12},{12,10},{14,16},{16,14},{18... | collective-permute-start | bytes 516104 | tf_op jit(solution)/shard_map/ppermute | solution.py:375
  39.1 7.9 %collective-permute-start.9 = (f32[384,128]{1,0:T(8,128)S(1)}, f32[384,128]{1,0:T(8,128)S(1)}, u32[]{:S(2)}, u32[]{:S(2)}) collective-permute-start(f32[384,128]{1,0:T(8,128)S(1)} %pad_maximum_fusion.8), channel_id=1, source_target_pairs={{0,1},{1,0},{2,3},{3,2},{4,5},{5,4},{6,7},{7,6},{8,9},{9,8},{10,11... | collective-permute-start | bytes 589832 | tf_op jit(solution)/shard_map/ppermute | solution.py:379
  40.7 14.0 %collective-permute-start.2 = (f32[2,4,128,128]{3,2,1,0:T(8,128)S(1)}, f32[2,4,128,128]{3,2,1,0:T(8,128)S(1)}, u32[]{:S(2)}, u32[]{:S(2)}) collective-permute-start(f32[2,4,128,128]{3,2,1,0:T(8,128)S(1)} %copy-done.8), channel_id=1, source_target_pairs={{0,1},{1,0},{2,3},{3,2},{4,5},{5,4},{6,7},{7,6},{8,9},{9,8},{10,11... | collective-permute-start | bytes 1572872 | tf_op jit(solution)/shard_map/ppermute | solution.py:379
  47.1 7.6 %collective-permute-start.10 = (f32[328,128]{1,0:T(8,128)S(1)}, f32[328,128]{1,0:T(8,128)S(1)}, u32[]{:S(2)}, u32[]{:S(2)}) collective-permute-start(f32[328,128]{1,0:T(8,128)S(1)} %pad_maximum_fusion.10), channel_id=1, source_target_pairs={{0,2},{2,0},{4,6},{6,4},{8,10},{10,8},{12,14},{14,12},{16,18},{18,... | collective-permute-start | bytes 503816 | tf_op jit(solution)/shard_map/ppermute | solution.py:369
  47.2 7.5 %collective-permute-start = (s32[2,4]{1,0:T(2,128)S(1)}, s32[2,4]{1,0:T(2,128)S(1)}, u32[]{:S(2)}, u32[]{:S(2)}) collective-permute-start(s32[2,4]{1,0:T(2,128)S(1)} %copy-done.11), channel_id=1, source_target_pairs={{0,1},{1,0},{2,3},{3,2},{4,5},{5,4},{6,7},{7,6},{8,9},{9,8},{10,11... | collective-permute-start | bytes 104 | tf_op jit(solution)/shard_map/ppermute | solution.py:379
  54.7 18.6 %copy-start.5 = (bf16[1280,768]{1,0:T(8,128)(2,1)S(1)}, bf16[1280,768]{1,0:T(8,128)(2,1)}, u32[]{:S(2)}) copy-start(bf16[1280,768]{1,0:T(8,128)(2,1)} %copy-done.4) | copy-start | bytes 5898244
  54.7 18.6 %copy-start.7 = (bf16[1280,768]{1,0:T(8,128)(2,1)S(1)}, bf16[1280,768]{1,0:T(8,128)(2,1)}, u32[]{:S(2)}) copy-start(bf16[1280,768]{1,0:T(8,128)(2,1)} %copy-done.6) | copy-start | bytes 5898244
  60.1 13.2 %copy-start.3 = (bf16[768,1280]{1,0:T(8,128)(2,1)S(1)}, bf16[768,1280]{1,0:T(8,128)(2,1)}, u32[]{:S(2)}) copy-start(bf16[768,1280]{1,0:T(8,128)(2,1)} %copy-done.2) | copy-start | bytes 5898244
  60.1 1.5 %collective-permute-start.11 = (f32[328,128]{1,0:T(8,128)S(1)}, f32[328,128]{1,0:T(8,128)S(1)}, u32[]{:S(2)}, u32[]{:S(2)}) collective-permute-start(f32[328,128]{1,0:T(8,128)S(1)} %get-tuple-element.38), channel_id=1, source_target_pairs={{0,2},{2,0},{4,6},{6,4},{8,10},{10,8},{12,14},{14,12},{16,18},{18,... | collective-permute-start | bytes 503816 | tf_op jit(solution)/shard_map/ppermute | solution.py:369
  61.7 9.5 %collective-permute-start.12 = (f32[656,128]{1,0:T(8,128)S(1)}, f32[656,128]{1,0:T(8,128)S(1)}, u32[]{:S(2)}, u32[]{:S(2)}) collective-permute-start(f32[656,128]{1,0:T(8,128)S(1)} %pad_maximum_fusion.1), channel_id=1, source_target_pairs={{0,30},{2,4},{4,2},{6,8},{8,6},{10,12},{12,10},{14,16},{16,14},{18... | collective-permute-start | bytes 1007624 | tf_op jit(solution)/shard_map/ppermute | solution.py:375
  71.3 2.0 %collective-permute-start.13 = (f32[328,128]{1,0:T(8,128)S(1)}, f32[328,128]{1,0:T(8,128)S(1)}, u32[]{:S(2)}, u32[]{:S(2)}) collective-permute-start(f32[328,128]{1,0:T(8,128)S(1)} %pad_maximum_fusion.11), channel_id=1, source_target_pairs={{0,2},{2,0},{4,6},{6,4},{8,10},{10,8},{12,14},{14,12},{16,18},{18,... | collective-permute-start | bytes 503816 | tf_op jit(solution)/shard_map/ppermute | solution.py:369
  78.4 1.5 %collective-permute-start.14 = (f32[328,128]{1,0:T(8,128)S(1)}, f32[328,128]{1,0:T(8,128)S(1)}, u32[]{:S(2)}, u32[]{:S(2)}) collective-permute-start(f32[328,128]{1,0:T(8,128)S(1)} %get-tuple-element.42), channel_id=1, source_target_pairs={{0,2},{2,0},{4,6},{6,4},{8,10},{10,8},{12,14},{14,12},{16,18},{18,... | collective-permute-start | bytes 503816 | tf_op jit(solution)/shard_map/ppermute | solution.py:369
  80.0 7.5 %collective-permute-start.17 = (f32[320,128]{1,0:T(8,128)S(1)}, f32[320,128]{1,0:T(8,128)S(1)}, u32[]{:S(2)}, u32[]{:S(2)}) collective-permute-start(f32[320,128]{1,0:T(8,128)S(1)} %fusion.11), channel_id=1, source_target_pairs={{0,30},{2,4},{4,2},{6,8},{8,6},{10,12},{12,10},{14,16},{16,14},{18... | collective-permute-start | bytes 491528 | tf_op jit(solution)/shard_map/ppermute | solution.py:375
  83.7 5.5 %collective-permute-start.15 = (f32[336,128]{1,0:T(8,128)S(1)}, f32[336,128]{1,0:T(8,128)S(1)}, u32[]{:S(2)}, u32[]{:S(2)}) collective-permute-start(f32[336,128]{1,0:T(8,128)S(1)} %fusion.5), channel_id=1, source_target_pairs={{0,1},{1,0},{2,3},{3,2},{4,5},{5,4},{6,7},{7,6},{8,9},{9,8},{10,11... | collective-permute-start | bytes 516104 | tf_op jit(solution)/shard_map/ppermute | solution.py:379
  89.2 7.6 %collective-permute-start.16 = (f32[336,128]{1,0:T(8,128)S(1)}, f32[336,128]{1,0:T(8,128)S(1)}, u32[]{:S(2)}, u32[]{:S(2)}) collective-permute-start(f32[336,128]{1,0:T(8,128)S(1)} %add.93), channel_id=1, source_target_pairs={{0,30},{2,4},{4,2},{6,8},{8,6},{10,12},{12,10},{14,16},{16,14},{18... | collective-permute-start | bytes 516104 | tf_op jit(solution)/shard_map/ppermute | solution.py:375
  91.2 5.7 %collective-permute-start.18 = (f32[384,128]{1,0:T(8,128)S(1)}, f32[384,128]{1,0:T(8,128)S(1)}, u32[]{:S(2)}, u32[]{:S(2)}) collective-permute-start(f32[384,128]{1,0:T(8,128)S(1)} %pad_maximum_fusion.9), channel_id=1, source_target_pairs={{0,1},{1,0},{2,3},{3,2},{4,5},{5,4},{6,7},{7,6},{8,9},{9,8},{10,11... | collective-permute-start | bytes 589832 | tf_op jit(solution)/shard_map/ppermute | solution.py:379
  97.0 1.5 %collective-permute-start.19 = (f32[328,128]{1,0:T(8,128)S(1)}, f32[328,128]{1,0:T(8,128)S(1)}, u32[]{:S(2)}, u32[]{:S(2)}) collective-permute-start(f32[328,128]{1,0:T(8,128)S(1)} %pad_maximum_fusion.12), channel_id=1, source_target_pairs={{0,2},{2,0},{4,6},{6,4},{8,10},{10,8},{12,14},{14,12},{16,18},{18,... | collective-permute-start | bytes 503816 | tf_op jit(solution)/shard_map/ppermute | solution.py:369
  103.5 2.3 %collective-permute-start.20 = (f32[392,128]{1,0:T(8,128)S(1)}, f32[392,128]{1,0:T(8,128)S(1)}, u32[]{:S(2)}, u32[]{:S(2)}) collective-permute-start(f32[392,128]{1,0:T(8,128)S(1)} %get-tuple-element.48), channel_id=1, source_target_pairs={{0,2},{2,0},{4,6},{6,4},{8,10},{10,8},{12,14},{14,12},{16,18},{18,... | collective-permute-start | bytes 602120 | tf_op jit(solution)/shard_map/ppermute | solution.py:369
  103.7 7.8 %collective-permute-start.21 = (f32[392,128]{1,0:T(8,128)S(1)}, f32[392,128]{1,0:T(8,128)S(1)}, u32[]{:S(2)}, u32[]{:S(2)}) collective-permute-start(f32[392,128]{1,0:T(8,128)S(1)} %get-tuple-element.47.edge), channel_id=1, source_target_pairs={{0,30},{2,4},{4,2},{6,8},{8,6},{10,12},{12,10},{14,16},{16,14},{18... | collective-permute-start | bytes 602120 | tf_op jit(solution)/shard_map/ppermute | solution.py:375
where the time goes:
time: 113 us; the launch traced here: 112 us
  waiting for transfers between devices  46.2 us (41%)
  starting transfers between devices  37 us (33%)
  Pallas kernels  23.3 us (21%)
  other arithmetic  2.47 us (2%)
  local copies, waits for them, and re-layouts  2.28 us (2%)
    ppermute x7, waiting for transfers between devices, to_edge(): return lax.ppermute(value, 'grid', route)  23.7 us
    ppermute x7, starting transfers between devices, to_edge(): return lax.ppermute(value, 'grid', route)  22.9 us
    ppermute x7, waiting for transfers between devices, to_orb(): return lax.ppermute(value, 'orb', [(0, 1), (1, 0)])  16.6 us
    ppermute x7, starting transfers between devices, to_orb(): return lax.ppermute(value, 'orb', [(0, 1), (1, 0)])  11.3 us
    pallas_call x2, Pallas kernels, shards(): whole_call(kernel, packed_outs, fock_scratch, 'fock', count=6 + len(opera...  10.5 us
    ppermute x8, waiting for transfers between devices, to_core(): return lax.ppermute(value, 'grid', [(i, i ^ 1) for i in range(count)])  5.88 us
    pallas_call x1, Pallas kernels, shards(): whole_call(functools.partial(domain_first, total_blocks), outs, [pltpu.VM...  5.35 us
    pallas_call x1, Pallas kernels, shards(): whole_call(functools.partial(domain_last, total_blocks), outs, [pltpu.VME...  4.94 us
  transfers between devices with their start and end apart: 22, of which 18 were waited for; matrix products, arithmetic and copies ran while one was open for 1% of the time, Pallas kernels for 2%

commit v1 on v0

--- a/solution.py
+++ b/solution.py
@@ -14,7 +14,7 @@
 TILE = 8
 HALF = NB // 2
 PACKED = NB + TILE
-VMEM_BYTES = 40 * 1024 * 1024
+VMEM_BYTES = 16 * 1024 * 1024
 POINT_CHUNK = 256
 f32 = jnp.float32
 bf16 = jnp.bfloat16
@@ -25,7 +25,6 @@
 B_ROWS = 2 * NB + HALF
 PAIR = PACKED + NB
 GIVE_ROWS = PAIR + HALF
-FINAL_ROWS = PAIR + NB
 
 
 def split(value):
@@ -112,17 +111,40 @@
     keep[...] = cross_ref[1 - core, pl.ds(aligned(core, HALF), HALF), :]
 
 
-def store_final(pair_ref, cross_ref, near, keep, give, edge):
+def store_final(pair_ref, cross_ref, turned_ref, own, give, edge):
     core = core_of()
-    places = ((1, near), (2 - 2 * core, give), (2 * core, edge))
-    for at, target in places:
-        merged, diagonal, off = pack_pair(pair_ref, at)
-        target[:NB, :] = merged
-        target[NB:PACKED, :] = diagonal
-        target[PACKED:PAIR, :] = off
-    give[PAIR:, :] = cross_ref[1 - core]
-    keep[...] = cross_ref[1 - core]
-    edge[PAIR:, :] = cross_ref[core]
+    half = aligned(lax.axis_index("orb"), HALF)
+    for j in range(2):
+        turned_ref[j] = cross_ref[j].T
+
+    def store_pair(at, target, first):
+        for i in range(2):
+            rows = pl.ds(half + i * NB, HALF)
+            for j in range(2):
+                index = 2 * i + j + 1 - first
+                target[index] = pair_ref[at, rows, j * NB : (j + 1) * NB]
+
+    def store_upper(target):
+        target[0] = turned_ref[1, pl.ds(half, HALF), :]
+        store_pair(2, target, 0)
+
+    def store_lower(target):
+        store_pair(0, target, 1)
+        target[4] = cross_ref[0, pl.ds(half, HALF), :]
+
+    own[0] = turned_ref[0, pl.ds(half, HALF), :]
+    store_pair(1, own, 0)
+    own[5] = cross_ref[1, pl.ds(half, HALF), :]
+
+    @pl.when(core == 0)
+    def _():
+        store_upper(give)
+        store_lower(edge)
+
+    @pl.when(core == 1)
+    def _():
+        store_lower(give)
+        store_upper(edge)
 
 
 def load_packed(side_a, side_b, mid, other):
@@ -193,20 +215,35 @@
 
 
 def fock_first(
-    weights, external, th, tl, nh, nl, own, edge, other,
-    out_a, out_b, give, keep, dens, sh, sl, pair_ref, cross_ref,
+    weights, external, th, tl, nh, nl, own, own_far, edge, edge_far, other, other_far,
+    out_a, out_b, give, keep, dens, sh, sl, pair_ref, cross_ref, ends_ref,
 ):
     core = core_of()
-    for i in range(2):
-        for j in range(2):
-            index = 3 * i + j - i + 1
-            rows, cols = slice(i * NB, (i + 1) * NB), slice(j * NB, (j + 1) * NB)
-            dens[1, rows, cols] = own[index]
-            dens[2 * core, rows, cols] = edge[index - 1 + core]
-            dens[2 - 2 * core, rows, cols] = other[index]
-    low = jnp.where(core == 0, edge[4], other[5])
-    high = jnp.where(core == 0, other[0], edge[0])
-    terms = [(1, 2, low), (2, 1, own[0]), (3, 4, own[5]), (4, 3, high)]
+    orb = lax.axis_index("orb")
+    for at, places in (
+        (1, ((own, 0, orb), (own_far, 0, 1 - orb))),
+        (2 * core, ((edge, 0, orb), (edge_far, 1 - core, 1 - orb))),
+        (2 - 2 * core, ((other, 0, orb), (other_far, 0, 1 - orb))),
+    ):
+        for source, first, half in places:
+            for i in range(2):
+                rows = pl.ds(aligned(half, HALF) + i * NB, HALF)
+                for j in range(2):
+                    index = 2 * i + j + 1 - first
+                    dens[at, rows, j * NB : (j + 1) * NB] = source[index]
+    ends = [
+        (0, edge, 5, edge_far, 4, other, 5, other_far, 5),
+        (1, own, 0, own_far, 0, own, 0, own_far, 0),
+        (2, own, 5, own_far, 5, own, 5, own_far, 5),
+        (3, other, 0, other_far, 0, edge, 0, edge_far, 0),
+    ]
+    mine = pl.ds(aligned(orb, HALF), HALF)
+    theirs = pl.ds(aligned(1 - orb, HALF), HALF)
+    for at, near_ref, a, near_far, b, far_ref, c, far_far, d in ends:
+        ends_ref[at, mine, :] = jnp.where(core == 0, near_ref[a], far_ref[c])
+        ends_ref[at, theirs, :] = jnp.where(core == 0, near_far[b], far_far[d])
+    places = ((1, 2), (2, 1), (3, 4), (4, 3))
+    terms = [(row, col, ends_ref[at]) for at, (row, col) in enumerate(places)]
     fock_body(
         weights, external, (th, tl), (nh, nl), dens, terms, (sh, sl), pair_ref, cross_ref
     )
@@ -215,7 +252,7 @@
 
 def fock_later(
     weights, external, th, tl, nh, nl, side_a, side_b, mid, other,
-    out_a, out_b, give, keep, dens, sh, sl, pair_ref, cross_ref,
+    out_a, out_b, give, keep, dens, sh, sl, pair_ref, cross_ref, ends_ref,
 ):
     rows, cols = row_col()
     core, pairs = load_packed(side_a, side_b, mid, other)
@@ -304,16 +341,17 @@
 
 
 def domain_first(
-    total_blocks, own_lists, other_lists, own, partner, side_a, side_b, mid, other,
+    total_blocks, own_lists, other_lists, own, partner, partner_last, side_a, side_b, mid, other,
     coef_out, out_a, out_b, give, keep, coef, gradient, moved, pair_ref, cross_ref,
 ):
     lists = [(own_lists, 0), (own_lists, 1), (other_lists, 0), (other_lists, 1)]
     coef[...] = jnp.zeros_like(coef)
     for d, (blocks, row) in enumerate(lists):
-        source = own if d < 2 else partner
         for i in range(4):
             at = aligned(relative(blocks[row, i], total_blocks), NB)
-            coef[pl.ds(at, NB), d * NB : (d + 1) * NB] = source[row, i]
+            coef[pl.ds(at, NB), d * NB : (d + 1) * NB] = (
+                own[row, i] if d < 2 else (partner, partner_last)[row][i]
+            )
     domain_body(
         total_blocks, lists, coef, side_a, side_b, mid, other,
         None, None, gradient, moved, pair_ref, cross_ref,
@@ -327,7 +365,7 @@
 
 def domain_last(
     total_blocks, own_lists, other_lists, coef, side_a, side_b, mid, other,
-    result, near, keep, give, edge, fresh, gradient, moved, pair_ref, cross_ref,
+    result, own, give, edge, fresh, gradient, moved, pair_ref, cross_ref, turned_ref,
 ):
     lists = [(own_lists, 0), (own_lists, 1), (other_lists, 0), (other_lists, 1)]
     domain_body(
@@ -340,28 +378,16 @@
         if d < 2:
             result[d, i] = value
     density_body(fresh, pair_ref, cross_ref)
-    store_final(pair_ref, cross_ref, near, keep, give, edge)
-
-
-def owner_kernel(near, keep, edge, from_core, from_edge, out, full):
+    store_final(pair_ref, cross_ref, turned_ref, own, give, edge)
+
+
+def owner_kernel(own, from_core, from_edge, out):
     core = core_of()
-    total = near[...] + from_core[:PAIR, :] + from_edge[:PAIR, :]
-    first, last = unpack_pair(total[:NB], total[NB : NB + 1])
-    off = total[PACKED:PAIR]
-    mid = keep[...] + from_core[PAIR:, :]
-    side = edge[PAIR:, :] + from_edge[PAIR:, :]
-    below = jnp.where(core == 0, side, mid)
-    above = jnp.where(core == 0, mid, side)
-    full[0, 0] = below.T
-    full[0, 1] = first
-    full[0, 2] = off
-    full[1, 0] = off.T
-    full[1, 1] = last
-    full[1, 2] = above
-    start = aligned(lax.axis_index("orb"), HALF)
-    for i in range(2):
-        for s in range(3):
-            out[i, s] = full[i, s, pl.ds(start, HALF), :]
+    lower = jnp.where(core == 0, from_core[...], from_edge[...])
+    upper = jnp.where(core == 0, from_edge[...], from_core[...])
+    out[0] = own[0] + upper[0]
+    out[1:5] = own[1:5] + upper[1:] + lower[:4]
+    out[5] = own[5] + lower[4]
 
 
 def to_core(value):
@@ -443,22 +469,23 @@
         moved=12 * points * window,
     )(batch_blocks, basis_values[0])
 
-    partner = to_orb(density)
-    first_half = lax.axis_index("orb") == 0
-    own = jnp.concatenate(
-        [jnp.where(first_half, density, partner), jnp.where(first_half, partner, density)], axis=2
-    ).reshape(6, NB, NB)
-    from_edge = to_edge(lax.dynamic_slice_in_dim(own, core, 5, 0))
-    from_core = to_core(own)
-    coefficients_ready, own = lax.optimization_barrier((coefficients, own))
-    other_coefficients = to_orb(coefficients_ready)
+    own = density.reshape(6, HALF, NB)
+    edge = to_edge(own)
+    own_far = to_orb(own)
+    other = to_core(own)
+    other_far = to_core(own_far)
+    edge_far = to_orb(lax.dynamic_slice_in_dim(edge, 1 - core, 5, 0))
+    window_density = (own, own_far, edge, edge_far, other, other_far)
+    coefficients_ready, edge_far = lax.optimization_barrier((coefficients, edge_far))
+    window_density = (own, own_far, edge, edge_far, other, other_far)
+    partner_coefficients = to_orb(coefficients_ready[0])
     other_lists = to_orb(domain_blocks)
 
     fock_scratch = [
         pltpu.VMEM((3, SB, SB), f32),
         pltpu.VMEM(full_shape, bf16),
         pltpu.VMEM(full_shape, bf16),
-    ] + band_scratch
+    ] + band_scratch + [pltpu.VMEM((4, NB, NB), f32)]
     domain_scratch = [pltpu.VMEM((window, 4 * NB), f32)] * 2 + band_scratch
     fock_cost = 2 * 3 * 8 * points * SB * SB
 
@@ -466,12 +493,18 @@
     packed = None
     for iteration in range(ITERS):
         if iteration == 0:
-            kernel, operands = fock_first, (own, from_edge, from_core)
+            kernel, operands = fock_first, window_density
         else:
             kernel, operands = fock_later, packed
         made = whole_call(
             kernel, packed_outs, fock_scratch, "fock", count=6 + len(operands), flops=fock_cost
         )(quad_weights, ext_potential, *basis, *operands)
+        if iteration == 0:
+            give, partner_coefficients, other_lists, rest = lax.optimization_barrier(
+                (made[2], partner_coefficients, other_lists, coefficients[1])
+            )
+            made = (made[0], made[1], give, made[3])
+            partner_last = to_orb(rest)
         packed = total_over_all(core, *made)
         if iteration < ITERS - 1:
             if iteration == 0:
@@ -482,18 +515,19 @@
                     [pltpu.VMEM((window, 4 * NB), f32)] + domain_scratch,
                     "domains",
                     smem=(0, 1),
-                    count=8,
+                    count=9,
                     flops=fock_cost // 2,
-                )(domain_blocks, other_lists, coefficients, other_coefficients, *packed)
+                )(domain_blocks, other_lists, coefficients, partner_coefficients, partner_last, *packed)
             packed = total_over_grid(core, *made)
         else:
-            outs = [(coefficients.shape, f32), ((PAIR, NB), f32), ((NB, NB), f32)] + [
-                ((FINAL_ROWS, NB), f32)
-            ] * 2
-            result, near, keep, give, edge = whole_call(
+            message = ((5, HALF, NB), f32)
+            outs = [(coefficients.shape, f32), ((6, HALF, NB), f32), message, message]
+            result, own, give, edge = whole_call(
                 functools.partial(domain_last, total_blocks),
                 outs,
-                [pltpu.VMEM((window, 4 * NB), f32)] + domain_scratch,
+                [pltpu.VMEM((window, 4 * NB), f32)]
+                + domain_scratch
+                + [pltpu.VMEM((2, NB, NB), f32)],
                 "domains_last",
                 smem=(0, 1),
                 count=7,
@@ -502,12 +536,9 @@
             arrived_edge = to_edge(edge)
             arrived_core = to_core(give)
             (rows,) = whole_call(
-                owner_kernel,
-                [(density.shape, f32)],
-                [pltpu.VMEM((2, 3, NB, NB), f32)],
-                "owner_rows",
-                count=5,
-            )(near, keep, edge, arrived_core, arrived_edge)
+                owner_kernel, [((6, HALF, NB), f32)], [], "owner_rows", count=3
+            )(own, arrived_core, arrived_edge)
+            rows = rows.reshape(density.shape)
     return (rows, result)
 
 

time: 113 us -> 109 us (0.965)
  waiting for transfers between devices: 46.2 us -> 40.2 us
  starting transfers between devices: 37 us -> 31.2 us
  local copies, waits for them, and re-layouts: 2.28 us -> 6.2 us
  other arithmetic: 2.47 us -> 5.47 us
  Pallas kernels: 23.3 us -> 24.5 us
    ppermute x7 -> x9, waiting for transfers between devices: 16.6 us -> 7.45 us  [to_orb(): return lax.ppermute(value, 'orb', [(0, 1), (1, 0)])]
    ppermute x7, starting transfers between devices: 22.9 us -> 18.7 us  [to_edge(): return lax.ppermute(value, 'grid', route)]
    unnamed x24 -> x32, local copies, waits for them, and re-layouts: 2.16 us -> 5.06 us
    ppermute x7, waiting for transfers between devices: 23.7 us -> 26.3 us  [to_edge(): return lax.ppermute(value, 'grid', route)]
    ppermute x7 -> x9, starting transfers between devices: 11.3 us -> 10.4 us  [to_orb(): return lax.ppermute(value, 'orb', [(0, 1), (1, 0)])]
    ppermute x8 -> x9, starting transfers between devices: 2.8 us -> 2.08 us  [to_core(): return lax.ppermute(value, 'grid', [(i, i ^ 1) for i in range(count)])]
    ppermute x8 -> x9, waiting for transfers between devices: 5.88 us -> 6.44 us  [to_core(): return lax.ppermute(value, 'grid', [(i, i ^ 1) for i in range(count)])]
  transfers between devices with their start and end apart: 22 -> 25, of which waited for: 18 -> 18; matrix products, arithmetic and copies ran while one was open for 1% -> 6% of each run, Pallas kernels for 2% -> 7%
where the time goes in v1:
time: 109 us
  waiting for transfers between devices  40.2 us (37%)
  starting transfers between devices  31.2 us (29%)
  Pallas kernels  24.5 us (22%)
  local copies, waits for them, and re-layouts  6.2 us (6%)
  other arithmetic  5.47 us (5%)
    ppermute x7, waiting for transfers between devices, to_edge(): return lax.ppermute(value, 'grid', route)  26.3 us
    ppermute x7, starting transfers between devices, to_edge(): return lax.ppermute(value, 'grid', route)  18.7 us
    pallas_call x2, Pallas kernels, shards(): whole_call(kernel, packed_outs, fock_scratch, 'fock', count=6 + len(opera...  11 us
    ppermute x9, starting transfers between devices, to_orb(): return lax.ppermute(value, 'orb', [(0, 1), (1, 0)])  10.4 us
    ppermute x9, waiting for transfers between devices, to_orb(): return lax.ppermute(value, 'orb', [(0, 1), (1, 0)])  7.45 us
    ppermute x9, waiting for transfers between devices, to_core(): return lax.ppermute(value, 'grid', [(i, i ^ 1) for i in range(count)])  6.44 us
    pallas_call x1, Pallas kernels, shards(): whole_call(functools.partial(domain_last, total_blocks), outs, [pltpu.VME...  5.75 us
    pallas_call x1, Pallas kernels, shards(): whole_call(functools.partial(domain_first, total_blocks), outs, [pltpu.VM...  5.35 us
  transfers between devices with their start and end apart: 25, of which 18 were waited for; matrix products, arithmetic and copies ran while one was open for 6% of the time, Pallas kernels for 7%

profile of v1, /device:TPU:0, one launch (start us, length us, event | category | flops | bytes accessed | tf_op | source)
XLA Modules:
  0.0 108.5 jit_solution(12725403244054136272)
XLA Ops:
  0.6 5.5 %collective-permute-start.1 = (f32[6,64,128]{2,1,0:T(8,128)}, f32[6,64,128]{2,1,0:T(8,128)S(1)}, u32[]{:S(2)}, u32[]{:S(2)}) collective-permute-start(f32[6,64,128]{2,1,0:T(8,128)} %bitcast.8), channel_id=1, source_target_pairs={{0,30},{2,4},{4,2},{6,8},{8,6},{10,12},{12,10},{14,16},{16,14},{18... | collective-permute-start | bytes 589832 | tf_op jit(solution)/shard_map/ppermute | solution.py:401
  6.1 1.5 %collective-permute-start = (f32[6,64,128]{2,1,0:T(8,128)}, f32[6,64,128]{2,1,0:T(8,128)S(1)}, u32[]{:S(2)}, u32[]{:S(2)}) collective-permute-start(f32[6,64,128]{2,1,0:T(8,128)} %bitcast.10), channel_id=1, source_target_pairs={{0,1},{1,0},{2,3},{3,2},{4,5},{5,4},{6,7},{7,6},{8,9},{9,8},{10,11... | collective-permute-start | bytes 589832 | tf_op jit(solution)/shard_map/ppermute | solution.py:405
  8.2 2.1 %copy-done = f32[1,1280,768]{2,1,0:T(8,128)S(1)} copy-done((f32[1,1280,768]{2,1,0:T(8,128)S(1)}, f32[1,1280,768]{2,1,0:T(8,128)}, u32[]{:S(2)}) %copy-start) | copy-done | bytes 3932184
  10.3 0.7 copy-done.2
  11.0 1.7 %sort_basis.1 = (bf16[768,1280]{1,0:T(8,128)(2,1)S(1)}, bf16[768,1280]{1,0:T(8,128)(2,1)S(1)}, bf16[1280,768]{1,0:T(8,128)(2,1)S(1)}, bf16[1280,768]{1,0:T(8,128)(2,1)S(1)}) custom-call(s32[1,6]{1,0:T(1,128)S(1)} %copy-done.2, f32[1280,768]{1,0:T(8,128)S(1)} %bitcast.7), custom_call_target="tpu_custom_call" | custom-call | bytes 11796480 | tf_op jit(solution)/shard_map/sort_basis/pallas_call | solution.py:462
  12.7 1.6 %collective-permute-start.2 = (f32[5,64,128]{2,1,0:T(8,128)S(1)}, f32[5,64,128]{2,1,0:T(8,128)S(1)}, u32[]{:S(2)}, u32[]{:S(2)}) collective-permute-start(f32[5,64,128]{2,1,0:T(8,128)S(1)} %constant_dynamic-slice_fusion.6), channel_id=1, source_target_pairs={{0,1},{1,0},{2,3},{3,2},{4,5},{5,4},{6,7},{7,6},{8,9},{9,8},{10,11... | collective-permute-start | bytes 491528 | tf_op jit(solution)/shard_map/ppermute | solution.py:405
  14.3 1.0 slice_bitcast_fusion
  15.3 0.7 copy-done.10
  16.0 2.9 %collective-permute-done.2.edge_far = f32[5,64,128]{2,1,0:T(8,128)S(1)} collective-permute-done((f32[5,64,128]{2,1,0:T(8,128)S(1)}, f32[5,64,128]{2,1,0:T(8,128)S(1)}, u32[]{:S(2)}, u32[]{:S(2)}) %collective-permute-start.2) | collective-permute-done | bytes 163872 | tf_op jit(solution)/shard_map/ppermute | solution.py:405
  18.9 1.6 %collective-permute-start.5 = (f32[4,128,128]{2,1,0:T(8,128)S(1)}, f32[4,128,128]{2,1,0:T(8,128)S(1)}, u32[]{:S(2)}, u32[]{:S(2)}) collective-permute-start(f32[4,128,128]{2,1,0:T(8,128)S(1)} %slice_bitcast_fusion.1), channel_id=1, source_target_pairs={{0,1},{1,0},{2,3},{3,2},{4,5},{5,4},{6,7},{7,6},{8,9},{9,8},{10,11... | collective-permute-start | bytes 786440 | tf_op jit(solution)/shard_map/ppermute | solution.py:405
  20.5 0.9 copy-done.11
  21.4 6.0 %fock.2 = (f32[336,128]{1,0:T(8,128)S(1)}, f32[320,128]{1,0:T(8,128)S(1)}, f32[328,128]{1,0:T(8,128)}, f32[64,128]{1,0:T(8,128)S(1)}) custom-call(f32[1,1280]{1,0:T(1,128)S(1)} %copy-done.12, f32[1,1280]{1,0:T(1,128)S(1)} %copy-done.13, bf16[768,1280]{1,0:T(8,128)(2,1)S(1)} %get-tuple-element.29.th, bf16[768,1280]{1,0:T(8,128)(2,1)S(1)} %get-tuple-element.30.tl, ...), custom_call_target="tpu_custom_call" | custom-call | flops 4026531840 | tf_op jit(solution)/shard_map/fock/pallas_call | solution.py:499
  27.5 1.6 %collective-permute-done.8 = f32[328,128]{1,0:T(8,128)S(1)} collective-permute-done((f32[328,128]{1,0:T(8,128)}, f32[328,128]{1,0:T(8,128)S(1)}, u32[]{:S(2)}, u32[]{:S(2)}) %collective-permute-start.8) | collective-permute-done | bytes 167968 | tf_op jit(solution)/shard_map/ppermute | solution.py:395
  29.8 1.7 %collective-permute-start.11 = (f32[320,128]{1,0:T(8,128)S(1)}, f32[320,128]{1,0:T(8,128)S(1)}, u32[]{:S(2)}, u32[]{:S(2)}) collective-permute-start(f32[320,128]{1,0:T(8,128)S(1)} %fusion.7), channel_id=1, source_target_pairs={{0,30},{2,4},{4,2},{6,8},{8,6},{10,12},{12,10},{14,16},{16,14},{18... | collective-permute-start | bytes 491528 | tf_op jit(solution)/shard_map/ppermute | solution.py:401
  31.5 0.9 slice_select_fusion.5
  32.4 1.3 %collective-permute-start.9 = (f32[336,128]{1,0:T(8,128)S(1)}, f32[336,128]{1,0:T(8,128)S(1)}, u32[]{:S(2)}, u32[]{:S(2)}) collective-permute-start(f32[336,128]{1,0:T(8,128)S(1)} %fusion.1), channel_id=1, source_target_pairs={{0,1},{1,0},{2,3},{3,2},{4,5},{5,4},{6,7},{7,6},{8,9},{9,8},{10,11... | collective-permute-start | bytes 516104 | tf_op jit(solution)/shard_map/ppermute | solution.py:405
  33.7 0.8 slice_add_fusion.8
  34.5 2.8 %collective-permute-done.11 = f32[320,128]{1,0:T(8,128)S(1)} collective-permute-done((f32[320,128]{1,0:T(8,128)S(1)}, f32[320,128]{1,0:T(8,128)S(1)}, u32[]{:S(2)}, u32[]{:S(2)}) %collective-permute-start.11) | collective-permute-done | bytes 163872 | tf_op jit(solution)/shard_map/ppermute | solution.py:401
  37.9 1.8 %collective-permute-start.10 = (f32[336,128]{1,0:T(8,128)S(1)}, f32[336,128]{1,0:T(8,128)}, u32[]{:S(2)}, u32[]{:S(2)}) collective-permute-start(f32[336,128]{1,0:T(8,128)S(1)} %add.79), channel_id=1, source_target_pairs={{0,30},{2,4},{4,2},{6,8},{8,6},{10,12},{12,10},{14,16},{16,14},{18... | collective-permute-start | bytes 516104 | tf_op jit(solution)/shard_map/ppermute | solution.py:401
  39.7 0.7 pad_maximum_fusion.7
  40.4 1.1 %collective-permute-start.12 = (f32[384,128]{1,0:T(8,128)}, f32[384,128]{1,0:T(8,128)}, u32[]{:S(2)}, u32[]{:S(2)}) collective-permute-start(f32[384,128]{1,0:T(8,128)} %pad_maximum_fusion.7), channel_id=1, source_target_pairs={{0,1},{1,0},{2,3},{3,2},{4,5},{5,4},{6,7},{7,6},{8,9},{9,8},{10,11... | collective-permute-start | bytes 589832 | tf_op jit(solution)/shard_map/ppermute | solution.py:405
  41.5 0.9 collective-permute-start.7
  42.4 3.2 %collective-permute-done.10 = f32[336,128]{1,0:T(8,128)} collective-permute-done((f32[336,128]{1,0:T(8,128)S(1)}, f32[336,128]{1,0:T(8,128)}, u32[]{:S(2)}, u32[]{:S(2)}) %collective-permute-start.10) | collective-permute-done | bytes 172064 | tf_op jit(solution)/shard_map/ppermute | solution.py:401
  45.6 0.9 add.80.side_a
  46.6 1.9 %collective-permute-done.12 = f32[384,128]{1,0:T(8,128)} collective-permute-done((f32[384,128]{1,0:T(8,128)}, f32[384,128]{1,0:T(8,128)}, u32[]{:S(2)}, u32[]{:S(2)}) %collective-permute-start.12) | collective-permute-done | bytes 196640 | tf_op jit(solution)/shard_map/ppermute | solution.py:405
  48.5 0.9 slice_add_fusion.3.side_b
  49.5 0.8 slice_add_fusion.7.mid
  50.3 1.3 %collective-permute-done.7.partner_last = f32[4,128,128]{2,1,0:T(8,128)S(1)} collective-permute-done((f32[4,128,128]{2,1,0:T(8,128)}, f32[4,128,128]{2,1,0:T(8,128)S(1)}, u32[]{:S(2)}, u32[]{:S(2)}) %collective-permute-start.7) | collective-permute-done | bytes 262176 | tf_op jit(solution)/shard_map/ppermute | solution.py:405
  51.7 5.3 %domains.1 = (f32[768,512]{1,0:T(8,128)S(1)}, f32[336,128]{1,0:T(8,128)S(1)}, f32[320,128]{1,0:T(8,128)S(1)}, f32[328,128]{1,0:T(8,128)S(1)}, f32[64,128]{1,0:T(8,128)S(1)}) custom-call(s32[2,4]{1,0:T(2,128)S(1)} %copy-done.14, s32[2,4]{1,0:T(2,128)S(1)} %collective-permute-done.6.other_lists, f32[2,4,128,128]{3,2,1,0:T(8,128)S(1)} %copy-done.1, ...), custom_call_target="tpu_custom_call" | custom-call | flops 2013265920 | tf_op jit(solution)/shard_map/domains/pallas_call | solution.py:512
  57.3 1.2 %collective-permute-done.14 = f32[328,128]{1,0:T(8,128)S(1)} collective-permute-done((f32[328,128]{1,0:T(8,128)S(1)}, f32[328,128]{1,0:T(8,128)S(1)}, u32[]{:S(2)}, u32[]{:S(2)}) %collective-permute-start.14) | collective-permute-done | bytes 167968 | tf_op jit(solution)/shard_map/ppermute | solution.py:395
  58.7 2.7 %collective-permute-start.15 = (f32[656,128]{1,0:T(8,128)S(1)}, f32[656,128]{1,0:T(8,128)S(1)}, u32[]{:S(2)}, u32[]{:S(2)}) collective-permute-start(f32[656,128]{1,0:T(8,128)S(1)} %pad_maximum_fusion), channel_id=1, source_target_pairs={{0,30},{2,4},{4,2},{6,8},{8,6},{10,12},{12,10},{14,16},{16,14},{18... | collective-permute-start | bytes 1007624 | tf_op jit(solution)/shard_map/ppermute | solution.py:401
  61.4 6.7 %collective-permute-done.15 = f32[656,128]{1,0:T(8,128)S(1)} collective-permute-done((f32[656,128]{1,0:T(8,128)S(1)}, f32[656,128]{1,0:T(8,128)S(1)}, u32[]{:S(2)}, u32[]{:S(2)}) %collective-permute-start.15) | collective-permute-done | bytes 335904 | tf_op jit(solution)/shard_map/ppermute | solution.py:401
  68.3 1.0 collective-permute-start.16
  69.3 1.0 collective-permute-done.16.other
  70.3 5.0 %fock.3 = (f32[336,128]{1,0:T(8,128)S(1)}, f32[320,128]{1,0:T(8,128)S(1)}, f32[328,128]{1,0:T(8,128)S(1)}, f32[64,128]{1,0:T(8,128)S(1)}) custom-call(f32[1,1280]{1,0:T(1,128)S(1)} %copy-done.12, f32[1,1280]{1,0:T(1,128)S(1)} %copy-done.13, bf16[768,1280]{1,0:T(8,128)(2,1)S(1)} %get-tuple-element.29.th, bf16[768,1280]{1,0:T(8,128)(2,1)S(1)} %copy-done.4, ...), custom_call_target="tpu_custom_call" | custom-call | flops 4026531840 | tf_op jit(solution)/shard_map/fock/pallas_call | solution.py:499
  75.8 1.0 collective-permute-done.17
  76.8 2.7 %collective-permute-start.20 = (f32[320,128]{1,0:T(8,128)S(1)}, f32[320,128]{1,0:T(8,128)S(1)}, u32[]{:S(2)}, u32[]{:S(2)}) collective-permute-start(f32[320,128]{1,0:T(8,128)S(1)} %fusion.11), channel_id=1, source_target_pairs={{0,30},{2,4},{4,2},{6,8},{8,6},{10,12},{12,10},{14,16},{16,14},{18... | collective-permute-start | bytes 491528 | tf_op jit(solution)/shard_map/ppermute | solution.py:401
  79.6 0.9 collective-permute-start.18
  80.6 3.8 %collective-permute-done.20 = f32[320,128]{1,0:T(8,128)S(1)} collective-permute-done((f32[320,128]{1,0:T(8,128)S(1)}, f32[320,128]{1,0:T(8,128)S(1)}, u32[]{:S(2)}, u32[]{:S(2)}) %collective-permute-start.20) | collective-permute-done | bytes 163872 | tf_op jit(solution)/shard_map/ppermute | solution.py:401
  84.4 0.7 collective-permute-done.18
  85.1 2.0 %collective-permute-start.19 = (f32[336,128]{1,0:T(8,128)S(1)}, f32[336,128]{1,0:T(8,128)S(1)}, u32[]{:S(2)}, u32[]{:S(2)}) collective-permute-start(f32[336,128]{1,0:T(8,128)S(1)} %add.94), channel_id=1, source_target_pairs={{0,30},{2,4},{4,2},{6,8},{8,6},{10,12},{12,10},{14,16},{16,14},{18... | collective-permute-start | bytes 516104 | tf_op jit(solution)/shard_map/ppermute | solution.py:401
  87.2 0.9 collective-permute-start.21
  88.1 4.6 %collective-permute-done.19 = f32[336,128]{1,0:T(8,128)S(1)} collective-permute-done((f32[336,128]{1,0:T(8,128)S(1)}, f32[336,128]{1,0:T(8,128)S(1)}, u32[]{:S(2)}, u32[]{:S(2)}) %collective-permute-start.19) | collective-permute-done | bytes 172064 | tf_op jit(solution)/shard_map/ppermute | solution.py:401
  93.1 1.4 %collective-permute-done.22.other = f32[328,128]{1,0:T(8,128)S(1)} collective-permute-done((f32[328,128]{1,0:T(8,128)S(1)}, f32[328,128]{1,0:T(8,128)S(1)}, u32[]{:S(2)}, u32[]{:S(2)}) %collective-permute-start.22) | collective-permute-done | bytes 167968 | tf_op jit(solution)/shard_map/ppermute | solution.py:395
  94.5 5.8 %domains_last.1 = (f32[2,4,128,128]{3,2,1,0:T(8,128)}, f32[6,64,128]{2,1,0:T(8,128)S(1)}, f32[5,64,128]{2,1,0:T(8,128)S(1)}, f32[5,64,128]{2,1,0:T(8,128)S(1)}) custom-call(s32[2,4]{1,0:T(2,128)S(1)} %copy-done.14, s32[2,4]{1,0:T(2,128)S(1)} %collective-permute-done.6.other_lists, f32[768,512]{1,0:T(8,128)S(1)} %get-tuple-element.43.coef, ...), custom_call_target="tpu_custom_call" | custom-call | flops 2013265920 | tf_op jit(solution)/shard_map/domains_last/pallas_call | solution.py:525
  100.4 2.3 %collective-permute-start.24 = (f32[5,64,128]{2,1,0:T(8,128)S(1)}, f32[5,64,128]{2,1,0:T(8,128)S(1)}, u32[]{:S(2)}, u32[]{:S(2)}) collective-permute-start(f32[5,64,128]{2,1,0:T(8,128)S(1)} %get-tuple-element.54), channel_id=1, source_target_pairs={{0,30},{2,4},{4,2},{6,8},{8,6},{10,12},{12,10},{14,16},{16,14},{18... | collective-permute-start | bytes 491528 | tf_op jit(solution)/shard_map/ppermute | solution.py:401
  102.6 5.2 %collective-permute-done.24.from_edge = f32[5,64,128]{2,1,0:T(8,128)S(1)} collective-permute-done((f32[5,64,128]{2,1,0:T(8,128)S(1)}, f32[5,64,128]{2,1,0:T(8,128)S(1)}, u32[]{:S(2)}, u32[]{:S(2)}) %collective-permute-start.24) | collective-permute-done | bytes 163872 | tf_op jit(solution)/shard_map/ppermute | solution.py:401
  107.8 0.7 owner_rows.1
  (83 shorter events, 3.7 us)
Async XLA Ops:
  0.6 12.1 %collective-permute-start.1 = (f32[6,64,128]{2,1,0:T(8,128)}, f32[6,64,128]{2,1,0:T(8,128)S(1)}, u32[]{:S(2)}, u32[]{:S(2)}) collective-permute-start(f32[6,64,128]{2,1,0:T(8,128)} %bitcast.8), channel_id=1, source_target_pairs={{0,30},{2,4},{4,2},{6,8},{8,6},{10,12},{12,10},{14,16},{16,14},{18... | collective-permute-start | bytes 589832 | tf_op jit(solution)/shard_map/ppermute | solution.py:401
  6.1 14.3 %collective-permute-start.3 = (f32[6,64,128]{2,1,0:T(8,128)}, f32[6,64,128]{2,1,0:T(8,128)S(1)}, u32[]{:S(2)}, u32[]{:S(2)}) collective-permute-start(f32[6,64,128]{2,1,0:T(8,128)} %bitcast.9), channel_id=1, source_target_pairs={{0,2},{2,0},{4,6},{6,4},{8,10},{10,8},{12,14},{14,12},{16,18},{18,... | collective-permute-start | bytes 589832 | tf_op jit(solution)/shard_map/ppermute | solution.py:395
  6.1 9.2 %collective-permute-start = (f32[6,64,128]{2,1,0:T(8,128)}, f32[6,64,128]{2,1,0:T(8,128)S(1)}, u32[]{:S(2)}, u32[]{:S(2)}) collective-permute-start(f32[6,64,128]{2,1,0:T(8,128)} %bitcast.10), channel_id=1, source_target_pairs={{0,1},{1,0},{2,3},{3,2},{4,5},{5,4},{6,7},{7,6},{8,9},{9,8},{10,11... | collective-permute-start | bytes 589832 | tf_op jit(solution)/shard_map/ppermute | solution.py:405
  7.6 19.8 %collective-permute-start.6 = (s32[2,4]{1,0:T(2,128)}, s32[2,4]{1,0:T(2,128)S(1)}, u32[]{:S(2)}, u32[]{:S(2)}) collective-permute-start(s32[2,4]{1,0:T(2,128)} %own_lists.3), channel_id=1, source_target_pairs={{0,1},{1,0},{2,3},{3,2},{4,5},{5,4},{6,7},{7,6},{8,9},{9,8},{10,11... | collective-permute-start | bytes 104 | tf_op jit(solution)/shard_map/ppermute | solution.py:405
  8.2 2.1 %copy-start = (f32[1,1280,768]{2,1,0:T(8,128)S(1)}, f32[1,1280,768]{2,1,0:T(8,128)}, u32[]{:S(2)}) copy-start(f32[1,1280,768]{2,1,0:T(8,128)} %param.8) | copy-start | bytes 11796484
  10.3 0.7 copy-start.2
  10.9 3.4 %copy-start.1 = (f32[2,4,128,128]{3,2,1,0:T(8,128)S(1)}, f32[2,4,128,128]{3,2,1,0:T(8,128)}, u32[]{:S(2)}) copy-start(f32[2,4,128,128]{3,2,1,0:T(8,128)} %own.1) | copy-start | bytes 1572868
  10.9 9.5 %copy-start.9 = (f32[2,3,64,128]{3,2,1,0:T(8,128)S(1)}, f32[2,3,64,128]{3,2,1,0:T(8,128)}, u32[]{:S(2)}) copy-start(f32[2,3,64,128]{3,2,1,0:T(8,128)} %param.7) | copy-start | bytes 589828
  10.9 9.5 %copy-start.12 = (f32[1,1280]{1,0:T(1,128)S(1)}, f32[1,1280]{1,0:T(1,128)}, u32[]{:S(2)}) copy-start(f32[1,1280]{1,0:T(1,128)} %weights.3) | copy-start | bytes 15364
  10.9 9.5 %copy-start.13 = (f32[1,1280]{1,0:T(1,128)S(1)}, f32[1,1280]{1,0:T(1,128)}, u32[]{:S(2)}) copy-start(f32[1,1280]{1,0:T(1,128)} %external.3) | copy-start | bytes 15364
  12.7 14.7 %copy-start.3 = (bf16[768,1280]{1,0:T(8,128)(2,1)}, bf16[768,1280]{1,0:T(8,128)(2,1)S(1)}, u32[]{:S(2)}) copy-start(bf16[768,1280]{1,0:T(8,128)(2,1)S(1)} %get-tuple-element.30.tl) | copy-start | bytes 5898244
  12.7 14.7 %copy-start.5 = (bf16[1280,768]{1,0:T(8,128)(2,1)}, bf16[1280,768]{1,0:T(8,128)(2,1)S(1)}, u32[]{:S(2)}) copy-start(bf16[1280,768]{1,0:T(8,128)(2,1)S(1)} %get-tuple-element.31.nh) | copy-start | bytes 5898244
  12.7 14.7 %copy-start.7 = (bf16[1280,768]{1,0:T(8,128)(2,1)}, bf16[1280,768]{1,0:T(8,128)(2,1)S(1)}, u32[]{:S(2)}) copy-start(bf16[1280,768]{1,0:T(8,128)(2,1)S(1)} %get-tuple-element.32.nl) | copy-start | bytes 5898244
  12.7 6.1 %collective-permute-start.2 = (f32[5,64,128]{2,1,0:T(8,128)S(1)}, f32[5,64,128]{2,1,0:T(8,128)S(1)}, u32[]{:S(2)}, u32[]{:S(2)}) collective-permute-start(f32[5,64,128]{2,1,0:T(8,128)S(1)} %constant_dynamic-slice_fusion.6), channel_id=1, source_target_pairs={{0,1},{1,0},{2,3},{3,2},{4,5},{5,4},{6,7},{7,6},{8,9},{9,8},{10,11... | collective-permute-start | bytes 491528 | tf_op jit(solution)/shard_map/ppermute | solution.py:405
  15.3 5.1 %collective-permute-start.4 = (f32[6,64,128]{2,1,0:T(8,128)S(1)}, f32[6,64,128]{2,1,0:T(8,128)S(1)}, u32[]{:S(2)}, u32[]{:S(2)}) collective-permute-start(f32[6,64,128]{2,1,0:T(8,128)S(1)} %collective-permute-done.own_far), channel_id=1, source_target_pairs={{0,2},{2,0},{4,6},{6,4},{8,10},{10,8},{12,14},{14,12},{16,18},{18,... | collective-permute-start | bytes 589832 | tf_op jit(solution)/shard_map/ppermute | solution.py:395
  15.3 0.7 copy-start.10
  18.9 8.5 %collective-permute-start.5 = (f32[4,128,128]{2,1,0:T(8,128)S(1)}, f32[4,128,128]{2,1,0:T(8,128)S(1)}, u32[]{:S(2)}, u32[]{:S(2)}) collective-permute-start(f32[4,128,128]{2,1,0:T(8,128)S(1)} %slice_bitcast_fusion.1), channel_id=1, source_target_pairs={{0,1},{1,0},{2,3},{3,2},{4,5},{5,4},{6,7},{7,6},{8,9},{9,8},{10,11... | collective-permute-start | bytes 786440 | tf_op jit(solution)/shard_map/ppermute | solution.py:405
  20.5 0.9 copy-start.11
  27.4 1.7 %collective-permute-start.8 = (f32[328,128]{1,0:T(8,128)}, f32[328,128]{1,0:T(8,128)S(1)}, u32[]{:S(2)}, u32[]{:S(2)}) collective-permute-start(f32[328,128]{1,0:T(8,128)} %get-tuple-element.40), channel_id=1, source_target_pairs={{0,2},{2,0},{4,6},{6,4},{8,10},{10,8},{12,14},{14,12},{16,18},{18,... | collective-permute-start | bytes 503816 | tf_op jit(solution)/shard_map/ppermute | solution.py:395
  29.1 0.7 copy-start.15
  29.8 21.9 %copy-start.14 = (s32[2,4]{1,0:T(2,128)S(1)}, s32[2,4]{1,0:T(2,128)}, u32[]{:S(2)}) copy-start(s32[2,4]{1,0:T(2,128)} %own_lists.3) | copy-start | bytes 100
  29.8 7.5 %collective-permute-start.11 = (f32[320,128]{1,0:T(8,128)S(1)}, f32[320,128]{1,0:T(8,128)S(1)}, u32[]{:S(2)}, u32[]{:S(2)}) collective-permute-start(f32[320,128]{1,0:T(8,128)S(1)} %fusion.7), channel_id=1, source_target_pairs={{0,30},{2,4},{4,2},{6,8},{8,6},{10,12},{12,10},{14,16},{16,14},{18... | collective-permute-start | bytes 491528 | tf_op jit(solution)/shard_map/ppermute | solution.py:401
  32.4 5.5 %collective-permute-start.9 = (f32[336,128]{1,0:T(8,128)S(1)}, f32[336,128]{1,0:T(8,128)S(1)}, u32[]{:S(2)}, u32[]{:S(2)}) collective-permute-start(f32[336,128]{1,0:T(8,128)S(1)} %fusion.1), channel_id=1, source_target_pairs={{0,1},{1,0},{2,3},{3,2},{4,5},{5,4},{6,7},{7,6},{8,9},{9,8},{10,11... | collective-permute-start | bytes 516104 | tf_op jit(solution)/shard_map/ppermute | solution.py:405
  37.9 7.7 %collective-permute-start.10 = (f32[336,128]{1,0:T(8,128)S(1)}, f32[336,128]{1,0:T(8,128)}, u32[]{:S(2)}, u32[]{:S(2)}) collective-permute-start(f32[336,128]{1,0:T(8,128)S(1)} %add.79), channel_id=1, source_target_pairs={{0,30},{2,4},{4,2},{6,8},{8,6},{10,12},{12,10},{14,16},{16,14},{18... | collective-permute-start | bytes 516104 | tf_op jit(solution)/shard_map/ppermute | solution.py:401
  40.4 8.2 %collective-permute-start.12 = (f32[384,128]{1,0:T(8,128)}, f32[384,128]{1,0:T(8,128)}, u32[]{:S(2)}, u32[]{:S(2)}) collective-permute-start(f32[384,128]{1,0:T(8,128)} %pad_maximum_fusion.7), channel_id=1, source_target_pairs={{0,1},{1,0},{2,3},{3,2},{4,5},{5,4},{6,7},{7,6},{8,9},{9,8},{10,11... | collective-permute-start | bytes 589832 | tf_op jit(solution)/shard_map/ppermute | solution.py:405
  41.5 10.1 %collective-permute-start.7 = (f32[4,128,128]{2,1,0:T(8,128)}, f32[4,128,128]{2,1,0:T(8,128)S(1)}, u32[]{:S(2)}, u32[]{:S(2)}) collective-permute-start(f32[4,128,128]{2,1,0:T(8,128)} %slice_bitcast_fusion), channel_id=1, source_target_pairs={{0,1},{1,0},{2,3},{3,2},{4,5},{5,4},{6,7},{7,6},{8,9},{9,8},{10,11... | collective-permute-start | bytes 786440 | tf_op jit(solution)/shard_map/ppermute | solution.py:405
  50.3 1.5 %collective-permute-start.13 = (f32[328,128]{1,0:T(8,128)S(1)}, f32[328,128]{1,0:T(8,128)S(1)}, u32[]{:S(2)}, u32[]{:S(2)}) collective-permute-start(f32[328,128]{1,0:T(8,128)S(1)} %pad_maximum_fusion.9), channel_id=1, source_target_pairs={{0,2},{2,0},{4,6},{6,4},{8,10},{10,8},{12,14},{14,12},{16,18},{18,... | collective-permute-start | bytes 503816 | tf_op jit(solution)/shard_map/ppermute | solution.py:395
  51.7 18.6 %copy-start.6 = (bf16[1280,768]{1,0:T(8,128)(2,1)S(1)}, bf16[1280,768]{1,0:T(8,128)(2,1)}, u32[]{:S(2)}) copy-start(bf16[1280,768]{1,0:T(8,128)(2,1)} %copy-done.5) | copy-start | bytes 5898244
  51.7 18.6 %copy-start.8 = (bf16[1280,768]{1,0:T(8,128)(2,1)S(1)}, bf16[1280,768]{1,0:T(8,128)(2,1)}, u32[]{:S(2)}) copy-start(bf16[1280,768]{1,0:T(8,128)(2,1)} %copy-done.7) | copy-start | bytes 5898244
  57.1 13.2 %copy-start.4 = (bf16[768,1280]{1,0:T(8,128)(2,1)S(1)}, bf16[768,1280]{1,0:T(8,128)(2,1)}, u32[]{:S(2)}) copy-start(bf16[768,1280]{1,0:T(8,128)(2,1)} %copy-done.3) | copy-start | bytes 5898244
  57.1 1.5 %collective-permute-start.14 = (f32[328,128]{1,0:T(8,128)S(1)}, f32[328,128]{1,0:T(8,128)S(1)}, u32[]{:S(2)}, u32[]{:S(2)}) collective-permute-start(f32[328,128]{1,0:T(8,128)S(1)} %get-tuple-element.45), channel_id=1, source_target_pairs={{0,2},{2,0},{4,6},{6,4},{8,10},{10,8},{12,14},{14,12},{16,18},{18,... | collective-permute-start | bytes 503816 | tf_op jit(solution)/shard_map/ppermute | solution.py:395
  58.7 9.5 %collective-permute-start.15 = (f32[656,128]{1,0:T(8,128)S(1)}, f32[656,128]{1,0:T(8,128)S(1)}, u32[]{:S(2)}, u32[]{:S(2)}) collective-permute-start(f32[656,128]{1,0:T(8,128)S(1)} %pad_maximum_fusion), channel_id=1, source_target_pairs={{0,30},{2,4},{4,2},{6,8},{8,6},{10,12},{12,10},{14,16},{16,14},{18... | collective-permute-start | bytes 1007624 | tf_op jit(solution)/shard_map/ppermute | solution.py:401
  68.3 2.0 %collective-permute-start.16 = (f32[328,128]{1,0:T(8,128)S(1)}, f32[328,128]{1,0:T(8,128)S(1)}, u32[]{:S(2)}, u32[]{:S(2)}) collective-permute-start(f32[328,128]{1,0:T(8,128)S(1)} %pad_maximum_fusion.10), channel_id=1, source_target_pairs={{0,2},{2,0},{4,6},{6,4},{8,10},{10,8},{12,14},{14,12},{16,18},{18,... | collective-permute-start | bytes 503816 | tf_op jit(solution)/shard_map/ppermute | solution.py:395
  75.3 1.5 %collective-permute-start.17 = (f32[328,128]{1,0:T(8,128)S(1)}, f32[328,128]{1,0:T(8,128)S(1)}, u32[]{:S(2)}, u32[]{:S(2)}) collective-permute-start(f32[328,128]{1,0:T(8,128)S(1)} %get-tuple-element.49), channel_id=1, source_target_pairs={{0,2},{2,0},{4,6},{6,4},{8,10},{10,8},{12,14},{14,12},{16,18},{18,... | collective-permute-start | bytes 503816 | tf_op jit(solution)/shard_map/ppermute | solution.py:395
  76.8 7.5 %collective-permute-start.20 = (f32[320,128]{1,0:T(8,128)S(1)}, f32[320,128]{1,0:T(8,128)S(1)}, u32[]{:S(2)}, u32[]{:S(2)}) collective-permute-start(f32[320,128]{1,0:T(8,128)S(1)} %fusion.11), channel_id=1, source_target_pairs={{0,30},{2,4},{4,2},{6,8},{8,6},{10,12},{12,10},{14,16},{16,14},{18... | collective-permute-start | bytes 491528 | tf_op jit(solution)/shard_map/ppermute | solution.py:401
  79.6 5.5 %collective-permute-start.18 = (f32[336,128]{1,0:T(8,128)S(1)}, f32[336,128]{1,0:T(8,128)S(1)}, u32[]{:S(2)}, u32[]{:S(2)}) collective-permute-start(f32[336,128]{1,0:T(8,128)S(1)} %fusion.5), channel_id=1, source_target_pairs={{0,1},{1,0},{2,3},{3,2},{4,5},{5,4},{6,7},{7,6},{8,9},{9,8},{10,11... | collective-permute-start | bytes 516104 | tf_op jit(solution)/shard_map/ppermute | solution.py:405
  85.1 7.6 %collective-permute-start.19 = (f32[336,128]{1,0:T(8,128)S(1)}, f32[336,128]{1,0:T(8,128)S(1)}, u32[]{:S(2)}, u32[]{:S(2)}) collective-permute-start(f32[336,128]{1,0:T(8,128)S(1)} %add.94), channel_id=1, source_target_pairs={{0,30},{2,4},{4,2},{6,8},{8,6},{10,12},{12,10},{14,16},{16,14},{18... | collective-permute-start | bytes 516104 | tf_op jit(solution)/shard_map/ppermute | solution.py:401
  87.2 5.7 %collective-permute-start.21 = (f32[384,128]{1,0:T(8,128)S(1)}, f32[384,128]{1,0:T(8,128)S(1)}, u32[]{:S(2)}, u32[]{:S(2)}) collective-permute-start(f32[384,128]{1,0:T(8,128)S(1)} %pad_maximum_fusion.8), channel_id=1, source_target_pairs={{0,1},{1,0},{2,3},{3,2},{4,5},{5,4},{6,7},{7,6},{8,9},{9,8},{10,11... | collective-permute-start | bytes 589832 | tf_op jit(solution)/shard_map/ppermute | solution.py:405
  93.0 1.5 %collective-permute-start.22 = (f32[328,128]{1,0:T(8,128)S(1)}, f32[328,128]{1,0:T(8,128)S(1)}, u32[]{:S(2)}, u32[]{:S(2)}) collective-permute-start(f32[328,128]{1,0:T(8,128)S(1)} %pad_maximum_fusion.11), channel_id=1, source_target_pairs={{0,2},{2,0},{4,6},{6,4},{8,10},{10,8},{12,14},{14,12},{16,18},{18,... | collective-permute-start | bytes 503816 | tf_op jit(solution)/shard_map/ppermute | solution.py:395
  100.2 2.4 %collective-permute-start.23 = (f32[5,64,128]{2,1,0:T(8,128)S(1)}, f32[5,64,128]{2,1,0:T(8,128)S(1)}, u32[]{:S(2)}, u32[]{:S(2)}) collective-permute-start(f32[5,64,128]{2,1,0:T(8,128)S(1)} %get-tuple-element.53), channel_id=1, source_target_pairs={{0,2},{2,0},{4,6},{6,4},{8,10},{10,8},{12,14},{14,12},{16,18},{18,... | collective-permute-start | bytes 491528 | tf_op jit(solution)/shard_map/ppermute | solution.py:395
  100.4 7.4 %collective-permute-start.24 = (f32[5,64,128]{2,1,0:T(8,128)S(1)}, f32[5,64,128]{2,1,0:T(8,128)S(1)}, u32[]{:S(2)}, u32[]{:S(2)}) collective-permute-start(f32[5,64,128]{2,1,0:T(8,128)S(1)} %get-tuple-element.54), channel_id=1, source_target_pairs={{0,30},{2,4},{4,2},{6,8},{8,6},{10,12},{12,10},{14,16},{16,14},{18... | collective-permute-start | bytes 491528 | tf_op jit(solution)/shard_map/ppermute | solution.py:401
